TPU v7x, 128 devices: a whole 4x4x4 slice. The times are simulated.
128 devices in a mesh: lon: 32 (over z_hi, y, x), lat: 4 (over z_lo, core).
Axes of the slice: x: 4, y: 4, z: 4 (z_hi: 2, z_lo: 2; z = z_hi * 2 + z_lo), core: 2. Of those that a mesh axis runs over, the one named last changes fastest.
Arguments:
- tokens: bfloat16 [4, 48, 384, 512], P(None, 'lat', 'lon'), may hold values from -6 to 6
- grad_output: bfloat16 [4, 48, 384, 512], P(None, 'lat', 'lon'), may hold values from -6 to 6
- norm_gain: float32 [512], replicated, may hold values from 0.1 to 1.9
- norm_bias: float32 [512], replicated, may hold values from -3 to 3
- w_qkv: bfloat16 [512, 1536], replicated, may hold values from -0.25 to 0.25
- w_proj: bfloat16 [512, 512], replicated, may hold values from -0.25 to 0.25
- rel_bias: float32 [8, 759], replicated, may hold values from -3 to 246
Outputs:
- grad_tokens: bfloat16 [4, 48, 384, 512], P(None, 'lat', 'lon')
- grad_qkv_weight: float32 [512, 1536], replicated
- grad_proj_weight: float32 [512, 512], replicated
- grad_norm_gain: float32 [512], replicated
- grad_norm_bias: float32 [512], replicated
- grad_rel_bias: float32 [8, 759], replicated
All inputs are finite; a program needn't handle non-finite values.
Results may differ from a plain program's by a relative error of at most 0.014.
Values may be sent and summed in bfloat16 or wider, within the bound.
A program may use at most 128 MiB of HBM per device.

v0:
```python
import math

import jax
import jax.numpy as jnp
from jax import lax
from jax.sharding import PartitionSpec as P

WIN_LEV = 2
WIN_LAT = 6
WIN_LON = 12


norm_eps = 1e-05
masked_score = -1000000000.0


def passed_along(block, axis, distance):
    devices = range(lax.axis_size(axis))
    route = [((i - distance) % len(devices), i) for i in devices]
    return lax.ppermute(block, axis, route)


def one_hots(extent):
    positions = jnp.arange(extent, dtype=jnp.int32)
    offsets = jnp.arange(2 * extent - 1, dtype=jnp.int32)
    return (
        positions[None, :, None] - positions[:, None, None] + extent - 1 == offsets[None, None, :]
    ).astype(jnp.float32)


def to_windows(array, win_lev, win_lat, win_lon):
    levels, rows, cols, last_dim = array.shape
    shaped = array.reshape(
        levels // win_lev, win_lev, rows // win_lat, win_lat, cols // win_lon, win_lon, last_dim
    )
    return shaped.transpose(0, 2, 4, 1, 3, 5, 6).reshape(-1, win_lev * win_lat * win_lon, last_dim)


def from_windows(array, levels, rows, cols, win_lev, win_lat, win_lon):
    last_dim = array.shape[-1]
    shaped = array.reshape(
        levels // win_lev, rows // win_lat, cols // win_lon, win_lev, win_lat, win_lon, last_dim
    )
    return shaped.transpose(0, 3, 1, 4, 2, 5, 6).reshape(levels, rows, cols, last_dim)


def window_backward(x_win, g_win, region, norm_gain, norm_bias, w_qkv, w_proj, rel_bias):
    win_count, tok_win, model_width = x_win.shape
    head_count = rel_bias.shape[0]
    head_dim = model_width // head_count
    score_scale = 1.0 / math.sqrt(head_dim)
    hp = lax.Precision.HIGHEST
    f32 = jnp.float32
    x_full = x_win.astype(f32)
    average = jnp.mean(x_full, -1, keepdims=True)
    centred = x_full - average
    variance = jnp.mean(centred * centred, -1, keepdims=True)
    inv_std = lax.rsqrt(variance + norm_eps)
    x_hat = centred * inv_std
    normed = (x_hat * norm_gain + norm_bias).astype(jnp.bfloat16)
    flat_in = normed.reshape(win_count * tok_win, model_width)
    qkv_all = jnp.dot(flat_in, w_qkv, preferred_element_type=f32).astype(jnp.bfloat16)
    qkv_all = qkv_all.reshape(win_count, tok_win, 3, head_count, head_dim)
    query_h = qkv_all[:, :, 0]
    key_h = qkv_all[:, :, 1]
    value_h = qkv_all[:, :, 2]
    hot_lev = one_hots(WIN_LEV)
    hot_lat = one_hots(WIN_LAT)
    hot_lon = one_hots(WIN_LON)
    bias_table = rel_bias.reshape(head_count, 2 * WIN_LEV - 1, 2 * WIN_LAT - 1, 2 * WIN_LON - 1)
    bias_full = jnp.einsum(
        "hxyz,psx,qty,ruz->hpqrstu", bias_table, hot_lev, hot_lat, hot_lon, precision=hp
    )
    bias_full = bias_full.reshape(head_count, tok_win, tok_win)
    scores = (
        jnp.einsum("bihc,bjhc->bhij", query_h, key_h, preferred_element_type=f32) * score_scale
        + bias_full
    )
    allowed = region[:, None, :, None] == region[:, None, None, :]
    scores = jnp.where(allowed, scores, masked_score)
    row_max = jnp.max(scores, -1, keepdims=True)
    exp_scores = jnp.exp(scores - row_max)
    probs = exp_scores / jnp.sum(exp_scores, -1, keepdims=True)
    probs_b = probs.astype(jnp.bfloat16)
    attended = jnp.einsum("bhij,bjhc->bihc", probs_b, value_h, preferred_element_type=f32).astype(
        jnp.bfloat16
    )
    attended = attended.reshape(win_count * tok_win, model_width)
    grad_flat = g_win.reshape(win_count * tok_win, model_width)
    contract_rows = (((0,), (0,)), ((), ()))
    d_proj = lax.dot_general(attended, grad_flat, contract_rows, preferred_element_type=f32)
    contract_cols = (((1,), (1,)), ((), ()))
    g_att = lax.dot_general(grad_flat, w_proj, contract_cols, preferred_element_type=f32).astype(
        jnp.bfloat16
    )
    g_att = g_att.reshape(win_count, tok_win, head_count, head_dim)
    d_probs = jnp.einsum("bihc,bjhc->bhij", g_att, value_h, preferred_element_type=f32)
    d_value = jnp.einsum("bhij,bihc->bjhc", probs_b, g_att, preferred_element_type=f32).astype(
        jnp.bfloat16
    )
    d_scores = probs * (d_probs - jnp.sum(probs * d_probs, -1, keepdims=True))
    d_bias_sum = jnp.sum(d_scores, 0).reshape(
        head_count, WIN_LEV, WIN_LAT, WIN_LON, WIN_LEV, WIN_LAT, WIN_LON
    )
    d_table = jnp.einsum(
        "hpqrstu,psx,qty,ruz->hxyz", d_bias_sum, hot_lev, hot_lat, hot_lon, precision=hp
    )
    d_scaled = (d_scores * score_scale).astype(jnp.bfloat16)
    d_query = jnp.einsum("bhij,bjhc->bihc", d_scaled, key_h, preferred_element_type=f32).astype(
        jnp.bfloat16
    )
    d_key = jnp.einsum("bhij,bihc->bjhc", d_scaled, query_h, preferred_element_type=f32).astype(
        jnp.bfloat16
    )
    d_qkv = jnp.stack([d_query, d_key, d_value], 2).reshape(win_count * tok_win, 3 * model_width)
    d_wqkv = lax.dot_general(flat_in, d_qkv, contract_rows, preferred_element_type=f32)
    d_normed = lax.dot_general(d_qkv, w_qkv, contract_cols, preferred_element_type=f32)
    d_normed = d_normed.reshape(win_count, tok_win, model_width)
    d_gain = jnp.sum(d_normed * x_hat, (0, 1))
    d_beta = jnp.sum(d_normed, (0, 1))
    g_hat = d_normed * norm_gain
    d_branch = inv_std * (
        g_hat
        - jnp.mean(g_hat, -1, keepdims=True)
        - x_hat * jnp.mean(g_hat * x_hat, -1, keepdims=True)
    )
    return (
        d_branch.astype(jnp.bfloat16),
        (d_wqkv, d_proj, d_gain, d_beta, d_table.reshape(head_count, -1)),
    )


def shards(tokens, grad_output, norm_gain, norm_bias, w_qkv, w_proj, rel_bias):
    levels, lat_dev, lon_dev, model_width = tokens.shape
    half_lev, half_lat, half_lon = (WIN_LEV // 2, WIN_LAT // 2, WIN_LON // 2)
    moved = passed_along((tokens[:, :, :half_lon], grad_output[:, :, :half_lon]), "lon", -1)
    across_in = jnp.concatenate([tokens[:, :, half_lon:], moved[0]], 2)
    across_grad = jnp.concatenate([grad_output[:, :, half_lon:], moved[1]], 2)
    moved = passed_along((across_in[:, :half_lat], across_grad[:, :half_lat]), "lat", -1)
    shifted_in = jnp.concatenate([across_in[:, half_lat:], moved[0]], 1)
    shifted_grad = jnp.concatenate([across_grad[:, half_lat:], moved[1]], 1)
    shifted_in = jnp.roll(shifted_in, -half_lev, 0)
    shifted_grad = jnp.roll(shifted_grad, -half_lev, 0)
    lat_total = lat_dev * lax.axis_size("lat")
    row_ids = lax.axis_index("lat") * lat_dev + jnp.arange(lat_dev, dtype=jnp.int32)
    lat_wrap = ((row_ids + half_lat) % lat_total < half_lat).astype(jnp.int32)
    lev_wrap = ((jnp.arange(levels, dtype=jnp.int32) + half_lev) % levels < half_lev).astype(
        jnp.int32
    )
    region = jnp.broadcast_to(
        lev_wrap[:, None, None] * 2 + lat_wrap[None, :, None], (levels, lat_dev, lon_dev)
    )
    x_windows = to_windows(shifted_in, WIN_LEV, WIN_LAT, WIN_LON)
    g_windows = to_windows(shifted_grad, WIN_LEV, WIN_LAT, WIN_LON)
    r_windows = to_windows(region[..., None], WIN_LEV, WIN_LAT, WIN_LON)[..., 0]
    d_branch, grads = window_backward(
        x_windows, g_windows, r_windows, norm_gain, norm_bias, w_qkv, w_proj, rel_bias
    )
    branch_grid = from_windows(d_branch, levels, lat_dev, lon_dev, WIN_LEV, WIN_LAT, WIN_LON)
    branch_grid = jnp.roll(branch_grid, half_lev, 0)
    from_north = passed_along(branch_grid[:, lat_dev - half_lat :], "lat", 1)
    branch_grid = jnp.concatenate([from_north, branch_grid[:, : lat_dev - half_lat]], 1)
    from_west = passed_along(branch_grid[:, :, lon_dev - half_lon :], "lon", 1)
    branch_grid = jnp.concatenate([from_west, branch_grid[:, :, : lon_dev - half_lon]], 2)
    grad_tokens = (grad_output.astype(jnp.float32) + branch_grid.astype(jnp.float32)).astype(
        jnp.bfloat16
    )
    d_wqkv, d_proj, d_gain, d_beta, d_table = grads
    summed = lax.psum((d_wqkv, d_proj, d_gain, d_beta, d_table), ("lon", "lat"))
    token_total = levels * lat_dev * lon_dev * lax.axis_size("lat") * lax.axis_size("lon")
    factor = token_total ** (-0.5)
    return (
        grad_tokens,
        summed[0] * factor,
        summed[1] * factor,
        summed[2] * factor,
        summed[3] * factor,
        summed[4] * factor,
    )


def solution(mesh):
    return jax.shard_map(
        shards,
        mesh=mesh,
        in_specs=(
            P(None, "lat", "lon", None),
            P(None, "lat", "lon", None),
            P(),
            P(),
            P(),
            P(),
            P(),
        ),
        out_specs=(P(None, "lat", "lon", None), P(), P(), P(), P(), P()),
        check_vma=False,
    )
```

profile of v0, /device:TPU:1, one launch (start us, length us, event | category | flops | bytes accessed | tf_op | source)
XLA Modules:
  0.0 390.3 jit_solution(17443219459770322983)
XLA Ops:
  7.2 1.4 fusion.83
  8.6 9.1 %collective-permute-start = (bf16[4,12,6,512]{3,0,2,1:T(4,128)(2,1)S(1)}, bf16[4,12,6,512]{3,0,2,1:T(4,128)(2,1)S(1)}, u32[]{:S(2)}, u32[]{:S(2)}) collective-permute-start(bf16[4,12,6,512]{3,0,2,1:T(4,128)(2,1)S(1)} %get-tuple-element.21), channel_id=1, source_target_pairs={{4,0},{8,4},{12,8},{16,12},{20,16},{24,20},{28,24},{32,28},{36,32}... | collective-permute-start | bytes 884744 | tf_op jit(solution)/shard_map/ppermute | solution.py:20
  17.7 1.3 fusion.84
  20.5 0.9 reshape.289
  21.4 1.1 fusion.61
  22.5 10.4 %convolution_bitcast_fusion.1 = f32[12,12,8,3,6,6,1]{1,5,4,3,2,0,6:T(8,128)S(1)} fusion(f32[12,12,8,3,11]{4,1,3,2,0:T(8,128)S(1)} %fusion.61, s32[6,6]{1,0:T(8,128)S(1)} %subtract_add_fusion.1), kind=kOutput, calls=%fused_computation.17 | convolution fusion | flops 16423308 | bytes 649872 | tf_op jit(solution)/shard_map/hxyz,psx,qty,ruz->hpqrstu/dot_general | solution.py:71
  32.9 13.7 %fusion.6 = f32[8,2,6,12,2,6,12]{6,4,1,5,2,0,3:T(2,128)} fusion(f32[12,12,8,3,6,6,1]{1,5,4,3,2,0,6:T(8,128)S(1)} %convolution_bitcast_fusion.1, s32[2,2]{1,0:T(2,128)S(1)} %copy-done.22), kind=kOutput, calls=%fused_computation.6 | convolution fusion | flops 5971980 | bytes 1161232 | tf_op jit(solution)/shard_map/hxyz,psx,qty,ruz->hpqrstu/dot_general | solution.py:71
  46.7 0.8 broadcast_compare_fusion
  47.5 15.6 %copy.117 = f32[8,2,6,12,2,6,12]{3,2,1,6,5,4,0:T(8,128)} copy(f32[8,2,6,12,2,6,12]{6,4,1,5,2,0,3:T(2,128)} %fusion.6) | data formatting | bytes 1327104 | tf_op jit(solution)/shard_map/add | solution.py:76
  63.1 7.5 %reshape.299 = f32[8,144,144]{1,2,0:T(8,128)} reshape(f32[8,2,6,12,2,6,12]{3,2,1,6,5,4,0:T(8,128)} %copy.117) | data formatting | bytes 1327104 | tf_op jit(solution)/shard_map/add | solution.py:76
  71.4 1.3 collective-permute-start.1
  73.5 2.7 collective-permute-done.1
  76.6 1.6 fusion.42
  78.2 2.6 reshape.285
  84.6 1.5 copy.144
  86.1 2.4 reshape.300
  88.6 2.4 reshape.283
  91.5 1.4 fusion.40
  93.0 1.9 reshape.275
  94.9 1.0 copy.145
  95.9 1.3 reshape_reshape.3
  97.2 2.4 convolution_convert_fusion.5
  99.5 2.5 reshape.303
  102.0 2.6 copy.83
  104.6 1.4 add_convert_fusion
  106.0 3.6 convolution_convert_fusion
  109.6 5.6 %reshape.302 = bf16[4,144,3,8,64]{4,3,2,1,0:T(8,128)(2,1)} reshape(bf16[576,1536]{1,0:T(8,128)(2,1)} %convolution_convert_fusion) | data formatting | bytes 3538944 | tf_op jit(solution)/shard_map/reshape | solution.py:63
  115.2 3.6 fusion.81
  118.8 2.6 copy.129
  121.4 2.6 copy.128
  123.9 1.6 copy.127
  125.6 4.7 %fusion.32 = f32[4,8,144,144]{2,3,1,0:T(8,128)} fusion(bf16[4,144,8,64]{1,3,2,0:T(8,128)(2,1)} %copy.83, bf16[4,144,1,8,64]{1,4,3,0,2:T(8,128)(2,1)} %copy.129), kind=kOutput, calls=%fused_computation.51 | convolution fusion | flops 84934656 | bytes 3833856 | tf_op jit(solution)/shard_map/bihc,bjhc->bhij/dot_general | solution.py:97
  130.2 0.8 fusion.35
  131.5 1.8 fusion.85
  133.3 1.9 fusion.24
  135.8 1.6 fusion.25
  137.4 9.1 %fusion.23 = bf16[4,144,1,8,64]{1,4,3,0,2:T(8,128)(2,1)} fusion(bf16[4,144,1,8,64]{1,4,3,0,2:T(8,128)(2,1)S(1)} %copy-done.5, f32[4,8,144,144]{2,3,1,0:T(8,128)} %fusion.32, f32[4,8,144,144]{2,3,1,0:T(8,128)} %copy-done.27, f32[4,8,144]{2,1,0:T(8,128)S(1)} %get-tuple-element.24), kind=kOutput, calls=%fused_computation.37 | convolution fusion | flops 89879184 | bytes 6506496 | tf_op jit(solution)/shard_map/bhij,bihc->bjhc/dot_general | solution.py:112
  146.5 8.3 %fusion.22 = bf16[4,144,1,8,64]{1,4,3,0,2:T(8,128)(2,1)S(1)} fusion(bf16[4,144,1,8,64]{1,4,3,0,2:T(8,128)(2,1)} %copy.127, f32[4,8,144,144]{2,3,1,0:T(8,128)} %fusion.32, f32[4,8,144,144]{2,3,1,0:T(8,128)} %copy-done.27, f32[4,8,144]{2,1,0:T(8,128)S(1)} %get-tuple-element.24), kind=kOutput, calls=%fused_computation.36 | convolution fusion | flops 89879184 | bytes 6506496 | tf_op jit(solution)/shard_map/bhij,bjhc->bihc/dot_general | solution.py:109
  154.8 9.0 %fusion.86 = f32[8,144,144]{1,2,0:T(8,128)} fusion(f32[4,8,144,144]{2,3,1,0:T(8,128)} %fusion.32, f32[4,8,144,144]{2,3,1,0:T(8,128)} %copy-done.27, f32[4,8,144]{2,1,0:T(8,128)S(1)} %get-tuple-element.24), kind=kOutput, calls=%fused_computation.130 | output fusion | flops 3820175 | bytes 5990400 | tf_op jit(solution)/shard_map/sub | solution.py:101
  163.8 0.7 pad_maximum_fusion
  164.5 1.7 copy-done.1
  166.2 4.5 %copy.93 = bf16[4,144,3,8,64]{1,0,4,3,2:T(4,128)(2,1)} copy(bf16[4,144,3,8,64]{1,4,3,0,2:T(8,128)(2,1)S(1)} %pad_maximum_fusion) | data formatting | bytes 3538944 | tf_op jit(solution)/shard_map/stack | solution.py:115
  170.7 6.4 %copy.88 = bf16[4,144,3,8,64]{4,3,2,1,0:T(8,128)(2,1)} copy(bf16[4,144,3,8,64]{1,4,3,0,2:T(8,128)(2,1)} %copy-done.1) | data formatting | bytes 3538944 | tf_op jit(solution)/shard_map/stack | solution.py:115
  177.1 0.9 convert_element_type.121
  178.1 2.0 copy.95
  180.1 1.5 reshape.280
  181.6 2.6 fusion.88
  184.3 6.4 %reshape.279 = bf16[576,1536]{0,1:T(8,128)(2,1)} reshape(bf16[4,144,3,8,64]{1,0,4,3,2:T(4,128)(2,1)} %copy.93) | data formatting | bytes 3538944 | tf_op jit(solution)/shard_map/reshape | solution.py:115
  190.7 5.9 %dot_general.63 = bf16[4,144,1536]{2,1,0:T(8,128)(2,1)} reshape(bf16[4,144,3,8,64]{4,3,2,1,0:T(8,128)(2,1)} %copy.88) | data formatting | bytes 3538944 | tf_op jit(solution)/shard_map/dot_general | solution.py:117
  196.5 3.0 multiply_reduce_fusion.2
  202.1 7.6 %reshape.301 = f32[8,2,6,12,2,6,12]{3,2,1,6,5,4,0:T(8,128)} reshape(f32[8,144,144]{1,2,0:T(8,128)} %fusion.86) | data formatting | bytes 1327104 | tf_op jit(solution)/shard_map/reshape | solution.py:102
  209.7 13.9 %copy.97 = f32[8,2,6,12,2,6,12]{6,4,1,5,3,2,0:T(2,128)} copy(f32[8,2,6,12,2,6,12]{3,2,1,6,5,4,0:T(8,128)} %reshape.301) | data formatting | bytes 1327104 | tf_op jit(solution)/shard_map/reshape | solution.py:102
  223.6 4.7 %fusion.87 = f32[512,1536]{1,0:T(8,128)} fusion(bf16[576,512]{1,0:T(8,128)(2,1)S(1)} %copy-done.13, bf16[576,1536]{0,1:T(8,128)(2,1)} %reshape.279), kind=kOutput, calls=%fused_computation.131 | convolution fusion | flops 905969664 | bytes 5505024 | tf_op jit(solution)/shard_map/dot_general | solution.py:116
  229.0 14.2 %convolution_bitcast_fusion = f32[3,8,6,12,6,12]{5,0,4,3,2,1:T(4,128)S(1)} fusion(f32[8,2,6,12,2,6,12]{6,4,1,5,3,2,0:T(2,128)} %copy.97, pred[2,2,3,1,1,1,1]{2,1,0,6,5,4,3:T(4,128)(4,1)S(1)} %copy-done.26), kind=kOutput, calls=%fused_computation.7 | convolution fusion | flops 5971968 | bytes 1161228 | tf_op jit(solution)/shard_map/hpqrstu,psx,qty,ruz->hxyz/dot_general | solution.py:105
  243.2 3.7 fusion.4
  246.9 1.1 fusion.28
  248.1 0.7 reshape.282
  248.8 63.0 %all-reduce = (f32[512]{0:T(512)S(1)}, f32[512]{0:T(512)S(1)}, f32[8,759]{1,0:T(8,128)S(1)}) all-reduce(f32[512]{0:T(512)S(1)} %get-tuple-element.6, f32[512]{0:T(512)S(1)} %get-tuple-element.9, f32[8,759]{1,0:T(8,128)} %reshape.282), channel_id=1, replica_groups=mesh['lon'=32,'lat'=4] {'lon','lat'}, use_global_device_ids=true, to_apply=%region_10.11 | all-reduce | flops 7096 | bytes 56768 | tf_op jit(solution)/shard_map/psum | solution.py:169
  312.5 0.9 collective-permute-start.5
  314.6 11.4 %collective-permute-done.5 = bf16[4,12,6,512]{3,0,2,1:T(4,128)(2,1)S(1)} collective-permute-done((bf16[4,12,6,512]{3,0,2,1:T(4,128)(2,1)S(1)}, bf16[4,12,6,512]{3,0,2,1:T(4,128)(2,1)S(1)}, u32[]{:S(2)}, u32[]{:S(2)}) %collective-permute-start.5) | collective-permute-done | bytes 294944 | tf_op jit(solution)/shard_map/ppermute | solution.py:20
  326.0 1.2 add_convert_fusion.1
  327.2 50.7 %all-reduce.4.cloned.1.call-done = (f32[512,1536]{1,0:T(8,128)}, f32[512,512]{1,0:T(8,128)}) async-done(((f32[512,1536]{1,0:T(8,128)}, f32[512,512]{1,0:T(8,128)}), (f32[512,1536]{1,0:T(8,128)}, f32[512,512]{1,0:T(8,128)})) %all-reduce.4.cloned.1.call-update) | async-done | bytes 4194320 | tf_op jit(solution)/shard_map/psum | solution.py:169
  377.9 4.0 %broadcast_multiply_fusion = f32[512,1536]{1,0:T(8,128)} fusion(f32[512,1536]{1,0:T(8,128)} %get-tuple-element.13), kind=kLoop, calls=%fused_computation.29 | loop fusion | flops 786432 | bytes 6291456 | tf_op jit(solution)/shard_map/mul | solution.py:174
  381.9 1.1 broadcast_multiply_fusion.1
  (100 shorter events, 14.1 us)
Async XLA Ops:
  7.2 98.8 %copy-start = (bf16[512,1536]{1,0:T(8,128)(2,1)S(1)}, bf16[512,1536]{1,0:T(8,128)(2,1)}, u32[]{:S(2)}) copy-start(bf16[512,1536]{1,0:T(8,128)(2,1)} %param.11) | copy-start | bytes 4718596
  7.2 370.7 %all-reduce.4.cloned.1.call-start = ((), (), s32[]{:S(2)}) async-start(), calls=%async_computation | async-start | bytes 8388608 | tf_op jit(solution)/shard_map/psum | solution.py:169
  8.6 62.7 %collective-permute-start = (bf16[4,12,6,512]{3,0,2,1:T(4,128)(2,1)S(1)}, bf16[4,12,6,512]{3,0,2,1:T(4,128)(2,1)S(1)}, u32[]{:S(2)}, u32[]{:S(2)}) collective-permute-start(bf16[4,12,6,512]{3,0,2,1:T(4,128)(2,1)S(1)} %get-tuple-element.21), channel_id=1, source_target_pairs={{4,0},{8,4},{12,8},{16,12},{20,16},{24,20},{28,24},{32,28},{36,32}... | collective-permute-start | bytes 884744 | tf_op jit(solution)/shard_map/ppermute | solution.py:20
  19.0 53.7 %collective-permute-start.2 = (bf16[4,12,6,512]{3,0,2,1:T(4,128)(2,1)S(1)}, bf16[4,12,6,512]{3,0,2,1:T(4,128)(2,1)S(1)}, u32[]{:S(2)}, u32[]{:S(2)}) collective-permute-start(bf16[4,12,6,512]{3,0,2,1:T(4,128)(2,1)S(1)} %get-tuple-element.23), channel_id=1, source_target_pairs={{4,0},{8,4},{12,8},{16,12},{20,16},{24,20},{28,24},{32,28},{36,32}... | collective-permute-start | bytes 884744 | tf_op jit(solution)/shard_map/ppermute | solution.py:20
  20.2 12.7 %copy-start.17 = (s32[6,6]{1,0:T(8,128)}, s32[6,6]{1,0:T(8,128)S(1)}, u32[]{:S(2)}) copy-start(s32[6,6]{1,0:T(8,128)S(1)} %subtract_add_fusion.1) | copy-start | bytes 436
  20.2 12.7 %copy-start.15 = (s32[12,12]{1,0:T(8,128)}, s32[12,12]{1,0:T(8,128)S(1)}, u32[]{:S(2)}) copy-start(s32[12,12]{1,0:T(8,128)S(1)} %subtract_add_fusion) | copy-start | bytes 1732
  22.5 10.4 %copy-start.22 = (s32[2,2]{1,0:T(2,128)S(1)}, s32[2,2]{1,0:T(2,128)}, u32[]{:S(2)}) copy-start(s32[2,2]{1,0:T(2,128)} %subtract_add_fusion.2) | copy-start | bytes 52
  71.4 4.8 %collective-permute-start.1 = (bf16[4,3,12,512]{3,0,2,1:T(4,128)(2,1)S(1)}, bf16[4,3,12,512]{3,0,2,1:T(4,128)(2,1)S(1)}, u32[]{:S(2)}, u32[]{:S(2)}) collective-permute-start(bf16[4,3,12,512]{3,0,2,1:T(4,128)(2,1)S(1)} %pad_maximum_fusion.6), channel_id=1, source_target_pairs={{1,0},{2,1},{3,2},{0,3},{5,4},{6,5},{7,6},{4,7},{9,8},{10,9},{11,1... | collective-permute-start | bytes 442376 | tf_op jit(solution)/shard_map/ppermute | solution.py:20
  72.8 18.2 %collective-permute-start.3 = (bf16[4,3,12,512]{3,0,2,1:T(4,128)(2,1)S(1)}, bf16[4,3,12,512]{3,0,2,1:T(4,128)(2,1)S(1)}, u32[]{:S(2)}, u32[]{:S(2)}) collective-permute-start(bf16[4,3,12,512]{3,0,2,1:T(4,128)(2,1)S(1)} %pad_maximum_fusion.5), channel_id=1, source_target_pairs={{1,0},{2,1},{3,2},{0,3},{5,4},{6,5},{7,6},{4,7},{9,8},{10,9},{11,1... | collective-permute-start | bytes 442376 | tf_op jit(solution)/shard_map/ppermute | solution.py:20
  99.5 5.1 %copy-start.21 = (f32[512]{0:T(512)S(1)}, f32[512]{0:T(512)}, u32[]{:S(2)}) copy-start(f32[512]{0:T(512)} %param.9) | copy-start | bytes 6148
  99.5 5.1 %copy-start.25 = (f32[512]{0:T(512)S(1)}, f32[512]{0:T(512)}, u32[]{:S(2)}) copy-start(f32[512]{0:T(512)} %param.10) | copy-start | bytes 6148
  102.0 3.9 %copy-start.23 = (f32[576]{0:T(1024)S(1)}, f32[576]{0:T(1024)}, u32[]{:S(2)}) copy-start(f32[576]{0:T(1024)} %div.26) | copy-start | bytes 6916
  102.0 3.9 %copy-start.24 = (f32[576]{0:T(1024)S(1)}, f32[576]{0:T(1024)}, u32[]{:S(2)}) copy-start(f32[576]{0:T(1024)} %rsqrt.18) | copy-start | bytes 6916
  125.6 4.7 %copy-start.5 = (bf16[4,144,1,8,64]{1,4,3,0,2:T(8,128)(2,1)S(1)}, bf16[4,144,1,8,64]{1,4,3,0,2:T(8,128)(2,1)}, u32[]{:S(2)}) copy-start(bf16[4,144,1,8,64]{1,4,3,0,2:T(8,128)(2,1)} %copy.128) | copy-start | bytes 1769476
  125.6 4.7 %copy-start.6 = (bf16[4,144,1,8,64]{1,4,3,0,2:T(8,128)(2,1)S(1)}, bf16[4,144,1,8,64]{1,4,3,0,2:T(8,128)(2,1)}, u32[]{:S(2)}) copy-start(bf16[4,144,1,8,64]{1,4,3,0,2:T(8,128)(2,1)} %copy.127) | copy-start | bytes 1769476
  130.2 1.3 copy-start.9
  130.2 1.3 copy-start.14
  131.5 1.8 copy-start.3
  133.3 2.5 copy-start.27
  133.3 2.5 copy-start.4
  154.8 9.0 %copy-start.11 = (bf16[4,144,1,8,64]{1,4,3,0,2:T(8,128)(2,1)S(1)}, bf16[4,144,1,8,64]{1,4,3,0,2:T(8,128)(2,1)}, u32[]{:S(2)}) copy-start(bf16[4,144,1,8,64]{1,4,3,0,2:T(8,128)(2,1)} %fusion.24) | copy-start | bytes 1769476
  154.8 9.0 %copy-start.12 = (bf16[4,144,1,8,64]{1,4,3,0,2:T(8,128)(2,1)S(1)}, bf16[4,144,1,8,64]{1,4,3,0,2:T(8,128)(2,1)}, u32[]{:S(2)}) copy-start(bf16[4,144,1,8,64]{1,4,3,0,2:T(8,128)(2,1)} %fusion.23) | copy-start | bytes 1769476
  164.5 1.7 copy-start.1
  170.7 6.4 %copy-start.7 = (bf16[2,2,1,2,6,12,512]{6,5,4,3,1,0,2:T(8,128)(2,1)S(1)}, bf16[2,2,1,2,6,12,512]{6,5,4,3,1,0,2:T(8,128)(2,1)}, u32[]{:S(2)}) copy-start(bf16[2,2,1,2,6,12,512]{6,5,4,3,1,0,2:T(8,128)(2,1)} %add_convert_fusion) | copy-start | bytes 1769476
  190.6 5.9 %copy-start.2 = (f32[4,144,512]{2,1,0:T(8,128)S(1)}, f32[4,144,512]{2,1,0:T(8,128)}, u32[]{:S(2)}) copy-start(f32[4,144,512]{2,1,0:T(8,128)} %reshape.300) | copy-start | bytes 3538948
  190.6 5.9 %copy-start.19 = (f32[4,144]{1,0:T(4,128)S(1)}, f32[4,144]{1,0:T(4,128)}, u32[]{:S(2)}) copy-start(f32[4,144]{1,0:T(4,128)} %div.30) | copy-start | bytes 6916
  190.7 5.9 %copy-start.20 = (f32[4,144]{1,0:T(4,128)S(1)}, f32[4,144]{1,0:T(4,128)}, u32[]{:S(2)}) copy-start(f32[4,144]{1,0:T(4,128)} %rsqrt.17) | copy-start | bytes 6916
  202.0 109.8 %collective-permute-start.4 = (bf16[4,3,12,512]{3,0,2,1:T(4,128)(2,1)S(1)}, bf16[4,3,12,512]{3,0,2,1:T(4,128)(2,1)S(1)}, u32[]{:S(2)}, u32[]{:S(2)}) collective-permute-start(bf16[4,3,12,512]{3,0,2,1:T(4,128)(2,1)S(1)} %pad_maximum_fusion.4), channel_id=1, source_target_pairs={{3,0},{0,1},{1,2},{2,3},{7,4},{4,5},{5,6},{6,7},{11,8},{8,9},{9,10... | collective-permute-start | bytes 442376 | tf_op jit(solution)/shard_map/ppermute | solution.py:20
  209.7 13.9 %copy-start.13 = (bf16[576,512]{1,0:T(8,128)(2,1)S(1)}, bf16[576,512]{1,0:T(8,128)(2,1)}, u32[]{:S(2)}) copy-start(bf16[576,512]{1,0:T(8,128)(2,1)} %convert_element_type.121) | copy-start | bytes 1769476
  228.3 0.7 copy-start.26
  229.0 14.2 %copy-start.18 = (s32[6,6]{1,0:T(8,128)S(1)}, s32[6,6]{1,0:T(8,128)}, u32[]{:S(2)}) copy-start(s32[6,6]{1,0:T(8,128)} %copy-done.17) | copy-start | bytes 436
  243.2 3.7 copy-start.16
  248.0 77.9 %copy-start.8 = (bf16[4,12,12,512]{3,0,2,1:T(4,128)(2,1)S(1)}, bf16[4,12,12,512]{3,0,2,1:T(4,128)(2,1)}, u32[]{:S(2)}) copy-start(bf16[4,12,12,512]{3,0,2,1:T(4,128)(2,1)} %param.8) | copy-start | bytes 1769476
  312.5 13.4 %collective-permute-start.5 = (bf16[4,12,6,512]{3,0,2,1:T(4,128)(2,1)S(1)}, bf16[4,12,6,512]{3,0,2,1:T(4,128)(2,1)S(1)}, u32[]{:S(2)}, u32[]{:S(2)}) collective-permute-start(bf16[4,12,6,512]{3,0,2,1:T(4,128)(2,1)S(1)} %get-tuple-element.18), channel_id=1, source_target_pairs={{124,0},{0,4},{4,8},{8,12},{12,16},{16,20},{20,24},{24,28},{28,32}... | collective-permute-start | bytes 884744 | tf_op jit(solution)/shard_map/ppermute | solution.py:20
  377.9 4.0 %copy-start.10 = (f32[512,512]{1,0:T(8,128)S(1)}, f32[512,512]{1,0:T(8,128)}, u32[]{:S(2)}) copy-start(f32[512,512]{1,0:T(8,128)} %get-tuple-element.14) | copy-start | bytes 3145732
Sparse Core Ops, SparseCore 0:
  228.4 149.4 all-reduce.3
where the time goes:
time: 398 us; the launch traced here: 390 us
  local copies, waits for them, and re-layouts  119 us (30%)
  matrix products  86.9 us (22%)
  waiting for transfers between devices  64.8 us (16%)
  blocking collectives  63 us (16%)
  other arithmetic  29.4 us (7%)
  between operations  15 us (4%)
  starting transfers between devices  12.1 us (3%)
    psum x1, blocking collectives, shards(): summed = lax.psum((d_wqkv, d_proj, d_gain, d_beta, d_table), ('lon', 'lat'))  63 us
    psum x1, waiting for transfers between devices, shards(): summed = lax.psum((d_wqkv, d_proj, d_gain, d_beta, d_table), ('lon', 'lat'))  50.7 us
    dot_general x3, matrix products, window_backward(): jnp.einsum('hxyz,psx,qty,ruz->hpqrstu', bias_table, hot_lev, hot_lat, hot...  25.2 us
    add x2, local copies, waits for them, and re-layouts, window_backward(): jnp.einsum('bihc,bjhc->bhij', query_h, key_h, preferred_element_type=f32)  23.1 us
    reshape x2, local copies, waits for them, and re-layouts, window_backward(): jnp.sum(d_scores, 0)  21.6 us
    dot_general x3, matrix products, window_backward(): jnp.einsum('hpqrstu,psx,qty,ruz->hxyz', d_bias_sum, hot_lev, hot_lat, hot...  19 us
    ppermute x6, waiting for transfers between devices, passed_along(): return lax.ppermute(block, axis, route)  14 us
    ppermute x6, starting transfers between devices, passed_along(): return lax.ppermute(block, axis, route)  12.1 us
  transfers between devices with their start and end apart: 7, of which 3 were waited for; matrix products, arithmetic and copies ran while one was open for 30% of the time, Pallas kernels for 0%

commit v1 on v0

v1 whole, which is shorter than its diff:
```python
import functools

import jax
import jax.numpy as jnp
from jax import lax
from jax.experimental import pallas as pl
from jax.experimental.pallas import tpu as pltpu
from jax.sharding import PartitionSpec as P

F32 = jnp.float32
BF16 = jnp.bfloat16
MESH = pl.DeviceIdType.MESH

NT = 144
WINS = 4
TOK = WINS * NT
D = 512
HEADS = 8
PAIRS = 4
RELS = 759
EPS = 1e-5
MASKED = -1e9
FACTOR = 73728 ** (-0.5)

PIECES = {
    "A": (0, 108, 112, 0, -1),
    "B": (112, 36, 48, -1, -1),
    "C": (160, 72, 80, -1, 0),
    "D": (240, 108, 112, 0, 1),
    "E": (352, 36, 48, -1, 1),
}
SEND_ROWS = 400
PLACES = {
    "A": ((0, 72, 72), (72, 36, 216)),
    "B": ((0, 36, 252),),
    "C": ((0, 36, 180), (36, 36, 540)),
    "D": ((0, 72, 288), (72, 36, 432)),
    "E": ((0, 36, 468),),
}


def half_slab(level, row, half):
    block, lev = {1: (0, 0), 2: (0, 1), 3: (1, 0), 0: (1, 1)}[level]
    off = lev * 18 + (row % 3) * 6
    own = half == 1 - block
    if row < 3:
        if own:
            return False, PIECES["C"][0] + 36 * block + off
        return False, PIECES["B" if block == 0 else "E"][0] + off
    north = (row - 3) // 3 * 36 if row < 9 else 0
    if own:
        return True, (2 * block + (row >= 9)) * NT + 72 * block + north + off
    base = PIECES["A" if block == 0 else "D"][0]
    return False, base + (72 if row >= 9 else north) + off


def place_of(i):
    o6 = i % 6
    a3 = i // 6 % 3
    lev = i // 18 % 2
    ah = i // 36 % 2
    oh = i // 72
    return 253 * lev + 23 * (3 * ah + a3) + 6 * oh + o6


def dot(a, b, precision=None):
    return lax.dot_general(
        a, b, (((1,), (0,)), ((), ())), precision=precision, preferred_element_type=F32
    )


def dot_nt(a, b):
    return lax.dot_general(a, b, (((1,), (1,)), ((), ())), preferred_element_type=F32)


def kernel(
    tok_hbm, grd_hbm, gain_ref, bias_ref, wqkv_hbm, wproj_hbm, rel_ref,
    out_tok, out_wqkv, out_wproj, out_gain, out_beta, out_table,
    tok, grd, wp, wproj, x32, g32, s32, inv, sndx, sndg, rcvx, rcvg, sndr, rcvr,
    normed, normt, qkv, gatt, gwin, dqkv, dn,
    tbl, sh, bj, bias_t, masks, dsum, dproj,
    cb, rc0, b1, rx, b2, ry, b3, rz, gb, ow, op,
    exb, exc, exx, exy, exz,
    load_sem, halo_s, halo_r, ret_s, ret_r, ars, arr, exs, exr, out_sem,
):
    lon = lax.axis_index("lon")
    lat = lax.axis_index("lat")
    core = lat % 2
    zz = (lon // 16) * 2 + lat // 2
    yy = (lon // 4) % 4
    xx = lon % 4

    def chip(z, y, x, c):
        return ((z // 2) * 16 + y * 4 + x, (z % 2) * 2 + c)

    def beside(dlat, dlon):
        return ((lon + dlon + 32) % 32, (lat + dlat + 4) % 4)

    def peer(axis, d):
        if axis == "x":
            return chip(zz, yy, (xx + d) % 4, core)
        if axis == "y":
            return chip(zz, (yy + d) % 4, xx, core)
        return chip((zz + d) % 4, yy, xx, core)

    other = chip(zz, yy, xx, 1 - core)

    barrier = pltpu.get_barrier_semaphore()
    greeted = [beside(a, o) for a in (-1, 0, 1) for o in (-1, 0, 1) if (a, o) != (0, 0)]
    greeted += [other] + [peer(axis, d) for axis in "xyz" for d in (1, 2, 3)]
    for device in greeted:
        pl.semaphore_signal(barrier, inc=1, device_id=device, device_id_type=MESH)

    loads = [
        pltpu.make_async_copy(tok_hbm, tok, load_sem.at[0]),
        pltpu.make_async_copy(grd_hbm, grd, load_sem.at[1]),
        pltpu.make_async_copy(wproj_hbm, wproj, load_sem.at[2]),
    ]
    for p in range(PAIRS):
        for s in range(3):
            loads.append(
                pltpu.make_async_copy(
                    wqkv_hbm.at[:, pl.ds(512 * s + 128 * p, 128)],
                    wp.at[:, pl.ds(384 * p + 128 * s, 128)],
                    load_sem.at[3 + 3 * p + s],
                )
            )
    for copy in loads:
        copy.start()

    def pack(source, mine, first):
        for level in (1, 2, 3, 0):
            for row in range(12):
                slab = source[level, row].astype(F32)
                for half in range(2):
                    own, at = half_slab(level, row, half)
                    piece = slab[6 * half : 6 * half + 6]
                    if own:
                        mine[at : at + 6, :] = piece
                    else:
                        s32[at : at + 6, :] = piece
        first[...] = s32[...].astype(BF16)

    def halo(k, name, src, dst):
        start, _, rows, dlat, dlon = PIECES[name]
        return pltpu.make_async_remote_copy(
            src_ref=src.at[pl.ds(start, rows)],
            dst_ref=dst.at[pl.ds(start, rows)],
            send_sem=halo_s.at[k],
            recv_sem=halo_r.at[k],
            device_id=beside(dlat, dlon),
            device_id_type=MESH,
        )

    xs = [halo(k, name, sndx, rcvx) for k, name in enumerate("ADBEC")]
    gs = [halo(5 + k, name, sndg, rcvg) for k, name in enumerate("ADBEC")]

    s32[...] = jnp.zeros((SEND_ROWS, D), F32)
    loads[0].wait()
    pack(tok, x32, sndx)
    pl.semaphore_wait(barrier, len(greeted))
    for copy in xs:
        copy.start()
    loads[1].wait()
    pack(grd, g32, sndg)
    for copy in gs:
        copy.start()

    tbl[...] = jnp.zeros((HEADS, 768), F32)
    tbl[:, 0:RELS] = rel_ref[...]
    table = tbl[...]
    for j in range(NT):
        at = place_of(j)
        turned = table if at == 0 else pltpu.roll(table, 768 - at, 1)
        sh[8 * j : 8 * j + 8, :] = turned[:, 0:384]

    def picks(shape, dim):
        lane = lax.broadcasted_iota(jnp.int32, shape, 1 - dim)
        place = jnp.where(lane < NT, 379 - place_of(lane), -1)
        return (lax.broadcasted_iota(jnp.int32, shape, dim) == place).astype(F32)

    spread = dot(sh[...], picks((384, 256), 0), lax.Precision.HIGHEST)
    for n in range(2):
        bj[n] = spread[:, 128 * n : 128 * n + 128]
    for h in range(HEADS):
        for n in range(2):
            bias_t[h, :, 128 * n : 128 * n + 128] = bj.at[n][pl.ds(h, NT, stride=8), :]

    ti = lax.broadcasted_iota(jnp.int32, (NT, 256), 0)
    tj = lax.broadcasted_iota(jnp.int32, (NT, 256), 1)
    lev_cut = (ti // 18) % 2 != (tj // 18) % 2
    lat_cut = ((ti // 36) % 2 != (tj // 36) % 2) & (lat == 3)
    masks[0] = jnp.where(lat_cut, MASKED, 0.0)
    masks[1] = jnp.where(lev_cut, MASKED, 0.0)
    masks[2] = jnp.where(lat_cut | lev_cut, MASKED, 0.0)

    def place(copies, source, mine):
        for copy, name in zip(copies, "ADBEC"):
            copy.wait_recv()
            start, _, rows, _, _ = PIECES[name]
            got = source[start : start + rows, :].astype(F32)
            for src, count, dst in PLACES[name]:
                mine[dst : dst + count, :] = got[src : src + count]

    place(xs, rcvx, x32)
    for copy in loads[2:]:
        copy.wait()
    gain = gain_ref[...]
    beta = bias_ref[...]

    def layer_norm(w, _):
        rows = pl.ds(pl.multiple_of(w * NT, NT), NT)
        x = x32[rows, :]
        centred = x - jnp.mean(x, -1, keepdims=True)
        variance = jnp.mean(centred * centred, -1, keepdims=True)
        scale = lax.rsqrt(variance + EPS)
        hat = centred * scale
        x32[rows, :] = hat
        inv[rows, :] = scale
        normed[rows, :] = (hat * gain + beta).astype(BF16)
        return 0

    lax.fori_loop(0, WINS, layer_norm, 0)
    normt[...] = normed[...].T

    def project(n, _):
        cols = pl.ds(pl.multiple_of(n * 256, 256), 256)
        qkv[:, cols] = dot(normed[...], wp[:, cols]).astype(BF16)
        return 0

    lax.fori_loop(0, 6, project, 0)

    place(gs, rcvg, g32)
    gwin[...] = g32[...].astype(BF16)

    def project_g(n, _):
        cols = pl.ds(pl.multiple_of(n * 256, 256), 256)
        gatt[:, cols] = dot_nt(gwin[...], wproj[cols, :]).astype(BF16)
        return 0

    lax.fori_loop(0, 2, project_g, 0)

    def ring(c, sem, axis, src_of, dst_of):
        copies = []
        for d in (1, 2, 3):
            copies.append(
                pltpu.make_async_remote_copy(
                    src_ref=src_of(d),
                    dst_ref=dst_of(d),
                    send_sem=ars.at[c, sem + d - 1],
                    recv_sem=arr.at[c, sem + d - 1],
                    device_id=peer(axis, d),
                    device_id_type=MESH,
                )
            )
        return copies

    def turned_to(at, d):
        return (at + d) % 4

    def rows_at(start, rows):
        return pl.ds(pl.multiple_of(start, 16), rows)

    def phase_copies(c, ph, arriving):
        sign = -1 if arriving else 1
        if ph in (0, 7):
            if ph == 0:
                src = cb.at[c, rows_at((1 - core) * 1024, 1024)]
                dst = rc0.at[c]
            else:
                src = gb.at[c, rows_at(core * 1024, 1024)]
                dst = gb.at[c, rows_at((1 - core if arriving else core) * 1024, 1024)]
            k = 0 if ph == 0 else 19
            return [
                pltpu.make_async_remote_copy(
                    src_ref=src, dst_ref=dst, send_sem=ars.at[c, k], recv_sem=arr.at[c, k],
                    device_id=other, device_id_type=MESH,
                )
            ]
        if ph == 1:
            return ring(c, 1, "x", lambda d: b1.at[c, rows_at(turned_to(xx, d) * 256, 256)], lambda d: rx.at[c, d - 1])
        if ph == 2:
            return ring(c, 4, "y", lambda d: b2.at[c, rows_at(turned_to(yy, d) * 64, 64)], lambda d: ry.at[c, d - 1])
        if ph == 3:
            return ring(c, 7, "z", lambda d: b3.at[c, rows_at(turned_to(zz, d) * 16, 16)], lambda d: rz.at[c, d - 1])

        def span(d):
            half = core * 1024
            x = xx if ph < 6 else (xx + d + 4) % 4
            y = yy if ph != 5 else (yy + d + 4) % 4
            z = zz if ph != 4 else (zz + d + 4) % 4
            if ph == 4:
                return rows_at(half + x * 256 + y * 64 + z * 16, 16)
            if ph == 5:
                return rows_at(half + x * 256 + y * 64, 64)
            return rows_at(half + x * 256, 256)

        axis = {4: "z", 5: "y", 6: "x"}[ph]
        sem = {4: 10, 5: 13, 6: 16}[ph]
        return ring(c, sem, axis, lambda d: gb.at[c, span(0)], lambda d: gb.at[c, span(-d if arriving else 0)])

    def send(c, ph):
        for copy in phase_copies(c, ph, False):
            copy.start()

    def receive(c, ph):
        for copy in phase_copies(c, ph, True):
            copy.wait_recv()
        if ph == 0:
            own = cb[c, rows_at(core * 1024, 1024), :].astype(F32)
            b1[c] = (own + rc0[c].astype(F32)).astype(BF16)
        elif ph in (1, 2, 3):
            src, got, at, rows = {1: (b1, rx, xx, 256), 2: (b2, ry, yy, 64), 3: (b3, rz, zz, 16)}[ph]
            own = src[c, rows_at(at * rows, rows), :].astype(F32)
            for d in range(3):
                own = own + got[c, d].astype(F32)
            own = own.astype(BF16)
            if ph == 1:
                b2[c] = own
            elif ph == 2:
                b3[c] = own
            else:
                gb[c, rows_at(core * 1024 + xx * 256 + yy * 64 + zz * 16, 16), :] = own
        elif ph == 7:
            for s in range(3):
                cols = pl.ds(pl.multiple_of(512 * s + c * 128, 128), 128)
                ow[:, cols] = gb[c, 512 * s : 512 * s + 512, :].astype(F32) * FACTOR
            rows = pl.ds(pl.multiple_of(c * 128, 128), 128)
            for n in range(4):
                part = gb[c, 1536 + 128 * n : 1664 + 128 * n, :]
                op[rows, 128 * n : 128 * n + 128] = part.astype(F32) * FACTOR

    def advance(c, k):
        receive(c, k - 1)
        if k < 8:
            send(c, k)

    low = lax.broadcasted_iota(jnp.int32, (NT, 128), 1) < 64

    def attend(p, w):
        rows = slice(w * NT, w * NT + NT)

        def cols(s):
            return pl.ds(pl.multiple_of(p * 384 + 128 * s, 128), 128)

        q = qkv[rows, cols(0)] * 0.125
        k = qkv[rows, cols(1)]
        v = qkv[rows, cols(2)]
        ga = gatt[rows, pl.ds(pl.multiple_of(p * 128, 128), 128)]
        kt = k.T
        vt = v.T
        zero = jnp.zeros((), BF16)
        att, dv, dk, dq = [], [], [], []
        for half in range(2):
            here = low if half == 0 else ~low
            kh = jnp.where(here, k, zero)
            vh = jnp.where(here, v, zero)
            lanes = slice(64 * half, 64 * half + 64)
            h = 2 * p + half
            s = dot_nt(kh, q) + bias_t[h][:, 0:NT]
            if w > 0:
                s = s + masks[w - 1][:, 0:NT]
            e = jnp.exp(s - jnp.max(s, 0, keepdims=True))
            prob = e * (1.0 / jnp.sum(e, 0, keepdims=True))
            pb = prob.astype(BF16)
            att.append(dot(vt[lanes], pb))
            dp = dot_nt(vh, ga)
            ds = prob * (dp - jnp.sum(prob * dp, 0, keepdims=True))
            if w == 0:
                dsum[h, :, 0:NT] = ds
            else:
                dsum[h, :, 0:NT] += ds
            db = ds.astype(BF16)
            dv.append(dot(pb, ga))
            dk.append(dot(db, q))
            dq.append(dot(kt[lanes], db) * 0.125)
        dqkv[rows, cols(0)] = jnp.concatenate(dq, 0).T.astype(BF16)
        dqkv[rows, cols(1)] = jnp.where(low, dk[0], dk[1]).astype(BF16)
        dqkv[rows, cols(2)] = jnp.where(low, dv[0], dv[1]).astype(BF16)
        part = dot(jnp.concatenate(att, 0).astype(BF16), gwin[rows, :])
        if w == 0:
            dproj[...] = part
        else:
            dproj[...] += part

    dsum[...] = jnp.zeros((HEADS, NT, 256), F32)

    def pair(p, _):
        for w in range(WINS):
            attend(p, w)
            if w == WINS - 1:
                grads = dot(normt[...], dqkv[:, pl.ds(pl.multiple_of(p * 384, 128), 384)])
                for s in range(3):
                    cb[p, 512 * s : 512 * s + 512, :] = grads[:, 128 * s : 128 * s + 128].astype(BF16)
                for n in range(4):
                    cb[p, 1536 + 128 * n : 1664 + 128 * n, :] = dproj[:, 128 * n : 128 * n + 128].astype(BF16)
                send(p, 0)

            @pl.when(p >= 1)
            def _():
                advance(p - 1, w + 1)

            @pl.when(p >= 2)
            def _():
                advance(p - 2, w + 5)

        return 0

    lax.fori_loop(0, PAIRS, pair, 0)

    def back(n, _):
        rows = pl.ds(pl.multiple_of(n * 256, 256), 256)
        dn[:, rows] = dot_nt(dqkv[...], wp[rows, :])
        return 0

    lax.fori_loop(0, 2, back, 0)
    advance(3, 1)
    advance(2, 5)

    def layer_norm_back(w, sums):
        rows = pl.ds(pl.multiple_of(w * NT, NT), NT)
        hat = x32[rows, :]
        d = dn[rows, :]
        dg = sums[0] + jnp.sum(d * hat, 0, keepdims=True)
        db = sums[1] + jnp.sum(d, 0, keepdims=True)
        g = d * gain
        m1 = jnp.mean(g, -1, keepdims=True)
        m2 = jnp.mean(g * hat, -1, keepdims=True)
        dn[rows, :] = inv[rows, :] * (g - m1 - hat * m2)
        return dg, db

    none = jnp.zeros((1, D), F32)
    dg, db = lax.fori_loop(0, WINS, layer_norm_back, (none, none))

    for name in PIECES:
        start = PIECES[name][0]
        for at, count, src in PLACES[name]:
            s32[start + at : start + at + count, :] = dn[src : src + count, :]
    sndr[...] = s32[...].astype(BF16)

    def homeward(k, name):
        start, _, rows, dlat, dlon = PIECES[name]
        return pltpu.make_async_remote_copy(
            src_ref=sndr.at[pl.ds(start, rows)],
            dst_ref=rcvr.at[pl.ds(start, rows)],
            send_sem=ret_s.at[k],
            recv_sem=ret_r.at[k],
            device_id=beside(-dlat, -dlon),
            device_id_type=MESH,
        )

    rets = [homeward(k, name) for k, name in enumerate("ADBEC")]
    for copy in rets:
        copy.start()

    advance(3, 2)
    advance(2, 6)

    for h in range(HEADS):
        for n in range(2):
            bj.at[n][pl.ds(h, NT, stride=8), :] = dsum[h, :, 128 * n : 128 * n + 128]
    sh[...] = dot(jnp.concatenate([bj[0], bj[1]], 1), picks((256, 384), 1), lax.Precision.HIGHEST)
    tbl[...] = jnp.zeros((HEADS, 768), F32)
    total = jnp.zeros((HEADS, 768), F32)
    rest = jnp.zeros((HEADS, 384), F32)
    for j in range(NT):
        at = place_of(j)
        wide = jnp.concatenate([sh[8 * j : 8 * j + 8, :], rest], 1)
        total = total + (wide if at == 0 else pltpu.roll(wide, at, 1))
    for n in range(6):
        exb[8 * n : 8 * n + 8, :] = total[:, 128 * n : 128 * n + 128]
    for n in range(4):
        exb[48 + n : 49 + n, :] = dg[:, 128 * n : 128 * n + 128]
        exb[52 + n : 53 + n, :] = db[:, 128 * n : 128 * n + 128]
    exb[56:64, :] = jnp.zeros((8, 128), F32)

    def small(k, src, dst, device):
        return pltpu.make_async_remote_copy(
            src_ref=src, dst_ref=dst, send_sem=exs.at[k], recv_sem=exr.at[k],
            device_id=device, device_id_type=MESH,
        )

    def small_ring(axis, at, buf, k, arriving):
        src = buf.at[at]
        out = []
        for d in (1, 2, 3):
            dst = buf.at[(at - d + 4) % 4 if arriving else at]
            out.append(small(k + d - 1, src, dst, peer(axis, d)))
        return out

    def small_step(axis, at, buf, k):
        for copy in small_ring(axis, at, buf, k, True):
            copy.wait_recv()
        return (buf[0] + buf[1]) + (buf[2] + buf[3])

    first = small(0, exb, exc, other)
    first.start()

    advance(3, 3)
    advance(2, 7)

    first.wait_recv()
    exx[xx] = exb[...] + exc[...]
    for copy in small_ring("x", xx, exx, 1, False):
        copy.start()

    advance(3, 4)
    advance(2, 8)

    exy[yy] = small_step("x", xx, exx, 1)
    for copy in small_ring("y", yy, exy, 4, False):
        copy.start()

    advance(3, 5)

    for copy in rets:
        copy.wait_recv()
    s32[...] = rcvr[...].astype(F32)
    for level in (1, 2, 3, 0):
        for row in range(12):
            halves = []
            for half in range(2):
                own, at = half_slab(level, row, half)
                buf = dn if own else s32
                halves.append(buf[at : at + 6, :].astype(BF16).astype(F32))
            both = jnp.concatenate(halves, 0)
            tok[level, row] = (grd[level, row].astype(F32) + both).astype(BF16)
    outs = [pltpu.make_async_copy(tok, out_tok, out_sem.at[0])]
    outs[0].start()

    exz[zz] = small_step("y", yy, exy, 4)
    for copy in small_ring("z", zz, exz, 7, False):
        copy.start()

    advance(3, 6)
    end = small_step("z", zz, exz, 7) * FACTOR
    for n in range(5):
        out_table[:, 128 * n : 128 * n + 128] = end[8 * n : 8 * n + 8]
    out_table[:, 640:RELS] = end[40:48, 0 : RELS - 640]
    for n in range(4):
        out_gain[:, 128 * n : 128 * n + 128] = end[48 + n : 49 + n]
        out_beta[:, 128 * n : 128 * n + 128] = end[52 + n : 53 + n]
    advance(3, 7)
    advance(3, 8)

    outs += [
        pltpu.make_async_copy(ow, out_wqkv, out_sem.at[1]),
        pltpu.make_async_copy(op, out_wproj, out_sem.at[2]),
    ]
    for copy in outs[1:]:
        copy.start()

    for copy in xs + gs + rets + [first]:
        copy.wait_send()
    for axis, at, buf, k in (("x", xx, exx, 1), ("y", yy, exy, 4), ("z", zz, exz, 7)):
        for copy in small_ring(axis, at, buf, k, False):
            copy.wait_send()

    def sent(c, _):
        for ph in range(8):
            for copy in phase_copies(c, ph, False):
                copy.wait_send()
        return 0

    lax.fori_loop(0, PAIRS, sent, 0)
    for copy in outs:
        copy.wait()


def shards(tokens, grad_output, norm_gain, norm_bias, w_qkv, w_proj, rel_bias):
    any_space = pl.BlockSpec(memory_space=pl.ANY)
    vmem = pl.BlockSpec(memory_space=pltpu.VMEM)
    dma = pltpu.SemaphoreType.DMA
    scratch = [
        pltpu.VMEM((4, 12, 12, D), BF16),
        pltpu.VMEM((4, 12, 12, D), BF16),
        pltpu.VMEM((D, 3 * D), BF16),
        pltpu.VMEM((D, D), BF16),
        pltpu.VMEM((TOK, D), F32),
        pltpu.VMEM((TOK, D), F32),
        pltpu.VMEM((SEND_ROWS, D), F32),
        pltpu.VMEM((TOK, 1), F32),
    ]
    scratch += [pltpu.VMEM((SEND_ROWS, D), BF16)] * 6
    scratch += [
        pltpu.VMEM((TOK, D), BF16),
        pltpu.VMEM((D, TOK), BF16),
        pltpu.VMEM((TOK, 3 * D), BF16),
        pltpu.VMEM((TOK, D), BF16),
        pltpu.VMEM((TOK, D), BF16),
        pltpu.VMEM((TOK, 3 * D), BF16),
        pltpu.VMEM((TOK, D), F32),
        pltpu.VMEM((HEADS, 768), F32),
        pltpu.VMEM((HEADS * NT, 384), F32),
        pltpu.VMEM((2, HEADS * NT, 128), F32),
        pltpu.VMEM((HEADS, NT, 256), F32),
        pltpu.VMEM((3, NT, 256), F32),
        pltpu.VMEM((HEADS, NT, 256), F32),
        pltpu.VMEM((128, D), F32),
        pltpu.VMEM((PAIRS, 2048, 128), BF16),
        pltpu.VMEM((PAIRS, 1024, 128), BF16),
        pltpu.VMEM((PAIRS, 1024, 128), BF16),
        pltpu.VMEM((PAIRS, 3, 256, 128), BF16),
        pltpu.VMEM((PAIRS, 256, 128), BF16),
        pltpu.VMEM((PAIRS, 3, 64, 128), BF16),
        pltpu.VMEM((PAIRS, 64, 128), BF16),
        pltpu.VMEM((PAIRS, 3, 16, 128), BF16),
        pltpu.VMEM((PAIRS, 2048, 128), BF16),
        pltpu.VMEM((D, 3 * D), F32),
        pltpu.VMEM((D, D), F32),
        pltpu.VMEM((64, 128), F32),
        pltpu.VMEM((64, 128), F32),
        pltpu.VMEM((4, 64, 128), F32),
        pltpu.VMEM((4, 64, 128), F32),
        pltpu.VMEM((4, 64, 128), F32),
        dma((15,)),
        dma((10,)),
        dma((10,)),
        dma((5,)),
        dma((5,)),
        dma((PAIRS, 20)),
        dma((PAIRS, 20)),
        dma((10,)),
        dma((10,)),
        dma((3,)),
    ]
    out = pl.pallas_call(
        kernel,
        out_shape=(
            jax.ShapeDtypeStruct(tokens.shape, BF16),
            jax.ShapeDtypeStruct((D, 3 * D), F32),
            jax.ShapeDtypeStruct((D, D), F32),
            jax.ShapeDtypeStruct((1, D), F32),
            jax.ShapeDtypeStruct((1, D), F32),
            jax.ShapeDtypeStruct((HEADS, RELS), F32),
        ),
        in_specs=[any_space, any_space, vmem, vmem, any_space, any_space, vmem],
        out_specs=(any_space, any_space, any_space, vmem, vmem, vmem),
        scratch_shapes=scratch,
        compiler_params=pltpu.CompilerParams(
            collective_id=0, has_side_effects=True, vmem_limit_bytes=56 * 1024 * 1024
        ),
    )(tokens, grad_output, norm_gain[None], norm_bias[None], w_qkv, w_proj, rel_bias)
    return out[0], out[1], out[2], out[3][0], out[4][0], out[5]


def solution(mesh):
    grid = P(None, "lat", "lon", None)
    return jax.shard_map(
        shards,
        mesh=mesh,
        in_specs=(grid, grid, P(), P(), P(), P(), P()),
        out_specs=(grid, P(), P(), P(), P(), P()),
        check_vma=False,
    )
```

time: 398 us -> 117 us (0.29); the launches traced: 390 us -> 117 us
  local copies, waits for them, and re-layouts: 119 us -> 13.2 us
  Pallas kernels: 0 us -> 103 us
  matrix products: 86.9 us -> 0 us
  waiting for transfers between devices: 64.8 us -> 0 us
  blocking collectives: 63 us -> 0 us
  other arithmetic: 29.4 us -> 0 us
  between operations: 15 us -> 0.65 us
  starting transfers between devices: 12.1 us -> 0 us
    pallas_call x0 -> x1, Pallas kernels: none -> 103 us  [shards(): pl.pallas_call(kernel, out_shape=(jax.ShapeDtypeStruct(tokens.shape, BF16...]
    dot_general x17 -> x0, matrix products: 86.9 us -> none  [the longest x3 25.2 us: window_backward(): jnp.einsum('hxyz,psx,qty,ruz->hpqrstu', bias_table, hot_lev, hot_lat, hot...]
    psum x1 -> x0, blocking collectives: 63 us -> none  [shards(): summed = lax.psum((d_wqkv, d_proj, d_gain, d_beta, d_table), ('lon', 'lat'))]
    psum x1 -> x0, waiting for transfers between devices: 50.7 us -> none  [shards(): summed = lax.psum((d_wqkv, d_proj, d_gain, d_beta, d_table), ('lon', 'lat'))]
    reshape x13 -> x0, local copies, waits for them, and re-layouts: 45 us -> none  [the longest x2 21.6 us: window_backward(): jnp.sum(d_scores, 0)]
    add x2 -> x0, local copies, waits for them, and re-layouts: 23.1 us -> none  [window_backward(): jnp.einsum('bihc,bjhc->bhij', query_h, key_h, preferred_element_type=f32)]
    ppermute x6 -> x0, waiting for transfers between devices: 14 us -> none  [passed_along(): return lax.ppermute(block, axis, route)]
    convert_element_type x7 -> x0, local copies, waits for them, and re-layouts: 12.4 us -> none  [the longest x4 8.97 us: window_backward(): x_full = x_win.astype(f32)]
  transfers between devices with their start and end apart: 7 -> 0, of which waited for: 3 -> 0; matrix products, arithmetic and copies ran while one was open for 30% -> 0% of each run, Pallas kernels for 0% -> 0%
where the time goes in v1:
time: 117 us
  Pallas kernels  103 us (88%)
  local copies, waits for them, and re-layouts  13.2 us (11%)
    pallas_call x1, Pallas kernels, shards(): pl.pallas_call(kernel, out_shape=(jax.ShapeDtypeStruct(tokens.shape, BF16...  103 us
    unnamed x16, local copies, waits for them, and re-layouts  13.2 us

profile of v1, /device:TPU:1, one launch (start us, length us, event | category | flops | bytes accessed | tf_op | source)
XLA Modules:
  0.0 116.5 jit_solution(11493035513985829224)
XLA Ops:
  0.6 2.1 %copy.13.tok_hbm = bf16[4,12,12,512]{3,2,1,0:T(8,128)(2,1)} copy(bf16[4,12,12,512]{3,0,2,1:T(4,128)(2,1)} %param.7) | data formatting | bytes 1179648 | tf_op args[0]
  2.7 2.1 %copy.14.grd_hbm = bf16[4,12,12,512]{3,2,1,0:T(8,128)(2,1)} copy(bf16[4,12,12,512]{3,0,2,1:T(4,128)(2,1)} %param.8) | data formatting | bytes 1179648 | tf_op args[1]
  4.8 102.7 %shard_map.118 = (bf16[4,12,12,512]{3,2,1,0:T(8,128)(2,1)}, f32[512,1536]{1,0:T(8,128)}, f32[512,512]{1,0:T(8,128)}, f32[1,512]{1,0:T(1,128)}, f32[1,512]{1,0:T(1,128)}, /*index=5*/f32[8,759]{1,0:T(8,128)}) custom-call(bf16[4,12,12,512]{3,2,1,0:T(8,128)(2,1)} %copy.13.tok_hbm, bf16[4,12,12,512]{3,2,1,0:T(8,128)(2,1)} %copy.14.grd_hbm, f32[1,512]{1,0:T(1,128)} %bitcast.4, ...), custom_call_target="tpu_custom_call" | custom-call | tf_op jit(solution)/shard_map/pallas_call | solution.py:627
  107.5 2.4 %copy.15 = bf16[4,12,12,512]{3,0,2,1:T(4,128)(2,1)} copy(bf16[4,12,12,512]{3,2,1,0:T(8,128)(2,1)} %get-tuple-element.18) | data formatting | bytes 1179648
  109.9 0.0 copy-start
  109.9 0.0 copy-start.3
  109.9 0.0 copy-start.2
  109.9 0.0 copy-start.1
  109.9 3.8 %copy.21 = f32[512,1536]{1,0:T(8,128)} copy(f32[512,1536]{1,0:T(8,128)} %get-tuple-element.31) | data formatting | bytes 6291456
  113.8 0.0 copy-done
  113.8 1.0 copy.22
  114.8 0.0 copy-done.3
  114.8 0.6 copy.23
  115.3 0.0 copy-done.2
  115.4 0.6 copy.24
  115.9 0.0 copy-done.1
  115.9 0.6 copy.25
Async XLA Ops:
  109.9 3.9 %copy-start = (f32[512,512]{1,0:T(8,128)S(1)}, f32[512,512]{1,0:T(8,128)}, u32[]{:S(2)}) copy-start(f32[512,512]{1,0:T(8,128)} %get-tuple-element.32) | copy-start | bytes 3145732
  109.9 4.8 %copy-start.3 = (f32[1,512]{1,0:T(1,128)S(1)}, f32[1,512]{1,0:T(1,128)}, u32[]{:S(2)}) copy-start(f32[1,512]{1,0:T(1,128)} %get-tuple-element.15) | copy-start | bytes 6148
  109.9 5.4 %copy-start.2 = (f32[1,512]{1,0:T(1,128)S(1)}, f32[1,512]{1,0:T(1,128)}, u32[]{:S(2)}) copy-start(f32[1,512]{1,0:T(1,128)} %get-tuple-element.16) | copy-start | bytes 6148
  109.9 6.0 %copy-start.1 = (f32[8,759]{1,0:T(8,128)S(1)}, f32[8,759]{1,0:T(8,128)}, u32[]{:S(2)}) copy-start(f32[8,759]{1,0:T(8,128)} %get-tuple-element.35) | copy-start | bytes 72868

commit v2 on v0

v2 whole, which is shorter than its diff:
```python
import functools

import jax
import jax.numpy as jnp
from jax import lax
from jax.experimental import pallas as pl
from jax.experimental.pallas import tpu as pltpu
from jax.sharding import PartitionSpec as P

F32 = jnp.float32
BF16 = jnp.bfloat16
MESH = pl.DeviceIdType.MESH

NT = 144
WINS = 4
TOK = WINS * NT
D = 512
HEADS = 8
PAIRS = 4
RELS = 759
EPS = 1e-5
MASKED = -1e9
FACTOR = 73728 ** (-0.5)

PIECES = (
    ((3, 6), (0, 6), (0, 1, 0, 6), 0, -1),
    ((9, 3), (6, 6), (1, 0, 0, 3), 0, 1),
    ((0, 3), (6, 6), (1, 0, 3, 3), -1, 1),
    ((0, 3), (0, 6), (1, 1, 3, 3), -1, 0),
)
KEPT = (
    ((3, 6), (6, 6), (0, 0, 0, 6)),
    ((9, 3), (0, 6), (1, 1, 0, 3)),
)
LEVELS = ((1, 2), (3, 0))


def place_of(i):
    o6 = i % 6
    a = i // 6 % 6
    oh = i // 36 % 2
    lev = i // 72
    return 253 * lev + 23 * a + 6 * oh + o6


STEPS = (
    (0, 4, "axis"),
    (0, 13, "plane"),
    (1, 11, "axis"),
    (2, 15, "axis"),
)


def dot(a, b, precision=None):
    return lax.dot_general(
        a, b, (((1,), (0,)), ((), ())), precision=precision, preferred_element_type=F32
    )


def dot_nt(a, b):
    return lax.dot_general(a, b, (((1,), (1,)), ((), ())), preferred_element_type=F32)


def kernel(
    tok_hbm, grd_hbm, gain_ref, bias_ref, wqkv_hbm, wproj_hbm, rel_ref,
    out_tok, out_sum, out_small,
    xw, gw, gnat, yw, ret, wp, wproj, x32, t32, inv,
    normed, normt, qkv, gatt, gwin, dqkv, dn,
    tbl, sh, bj, bias_t, masks, dsum, probs, atts,
    cb, rc0, b1, ra, r1, rs, gb,
    exb, exc, exx, exy, exz,
    load_sem, halo_s, halo_r, ret_s, ret_r, core_s, core_r, ax_s, ax_r, rs_s, rs_r, ag_s, ag_r, exs, exr, out_sem,
):
    lon = lax.axis_index("lon")
    lat = lax.axis_index("lat")
    core = lax.rem(lat, 2)
    zz = lax.div(lon, 16) * 2 + lax.div(lat, 2)
    flat = lax.rem(lon, 16)
    yy = lax.div(flat, 4)
    xx = lax.rem(flat, 4)
    me = zz * 16 + flat
    layer_lon = [lax.div(lax.rem(zz + d, 4), 2) * 16 for d in range(4)]
    layer_lat = [lax.rem(lax.rem(zz + d, 4), 2) * 2 + core for d in range(4)]

    def turned(at, d, count):
        return lax.rem(at + d, count)

    def beside(dlat, dlon):
        return (turned(lon, dlon + 32, 32), turned(lat, dlat + 4, 4))

    def peer(axis, d):
        if axis == "x":
            return (lon - xx + turned(xx, d, 4), lat)
        if axis == "y":
            return (lon - yy * 4 + turned(yy, d, 4) * 4, lat)
        return (layer_lon[d] + flat, layer_lat[d])

    other = (lon, lat + 1 - 2 * core)

    def all_chips(act):
        for dz in range(4):

            def one(d, _):
                r = turned(flat, d, 16)
                act((layer_lon[dz] + r, layer_lat[dz]), turned(zz, dz, 4) * 16 + r)
                return 0

            lax.fori_loop(1 if dz == 0 else 0, 16, one, 0)

    barrier = pltpu.get_barrier_semaphore()

    def greet(device):
        pl.semaphore_signal(barrier, inc=1, device_id=device, device_id_type=MESH)

    around = [beside(0, -1), beside(0, 1), beside(-1, 1), beside(1, -1), beside(-1, 0), beside(1, 0), other]
    for device in around:
        greet(device)
    all_chips(lambda device, _: greet(device))

    loads = []

    def load(src, dst):
        loads.append(pltpu.make_async_copy(src, dst, load_sem.at[len(loads)]))
        loads[-1].start()

    def grid_part(ref, rows, cols):
        return ref.at[pl.ds(*rows), pl.ds(*cols)]

    def window_part(ref, at):
        return ref.at[at[0], at[1], pl.ds(at[2], at[3])]

    for rows, cols, at in KEPT:
        load(grid_part(tok_hbm, rows, cols), window_part(xw, at))
    for p in range(PAIRS):
        for n in range(3):
            load(
                wqkv_hbm.at[:, pl.ds(512 * n + 128 * p, 128)],
                wp.at[:, pl.ds(384 * p + 128 * n, 128)],
            )
    for rows, cols, at in KEPT:
        load(grid_part(grd_hbm, rows, cols), window_part(gw, at))
    load(wproj_hbm, wproj)
    load(grd_hbm, gnat)

    def halo(k, piece, src, dst):
        rows, cols, at, dlat, dlon = piece
        return pltpu.make_async_remote_copy(
            src_ref=grid_part(src, rows, cols),
            dst_ref=window_part(dst, at),
            send_sem=halo_s.at[k],
            recv_sem=halo_r.at[k],
            device_id=beside(dlat, dlon),
            device_id_type=MESH,
        )

    xs = [halo(k, piece, tok_hbm, xw) for k, piece in enumerate(PIECES)]
    gs = [halo(4 + k, piece, grd_hbm, gw) for k, piece in enumerate(PIECES)]
    pl.semaphore_wait(barrier, 63 + len(around))
    for copy in xs:
        copy.start()

    tbl[...] = jnp.zeros((HEADS, 768), F32)
    tbl[:, 0:RELS] = rel_ref[...]
    table = tbl[...]
    for j in range(NT):
        at = place_of(j)
        shifted = table if at == 0 else pltpu.roll(table, 768 - at, 1)
        sh[8 * j : 8 * j + 8, :] = shifted[:, 0:384]

    def picks(shape, dim):
        lane = lax.broadcasted_iota(jnp.int32, shape, 1 - dim)
        place = jnp.where(lane < NT, 379 - place_of(lane), -1)
        return (lax.broadcasted_iota(jnp.int32, shape, dim) == place).astype(F32)

    spread = dot(sh[...], picks((384, 256), 0), lax.Precision.HIGHEST)
    for n in range(2):
        bj[n] = spread[:, 128 * n : 128 * n + 128]
    for h in range(HEADS):
        both = jnp.concatenate([bj.at[n][pl.ds(h, NT, stride=8), :] for n in range(2)], 1)
        bias_t[h // 2, :, NT * (h % 2) : NT * (h % 2) + NT] = both[:, 0:NT]

    ti = lax.broadcasted_iota(jnp.int32, (NT, 2 * NT), 0)
    tj = lax.broadcasted_iota(jnp.int32, (NT, 2 * NT), 1) % NT
    lev_cut = ti // 72 != tj // 72
    lat_cut = ((ti // 18) % 2 != (tj // 18) % 2) & (lat == 3)
    masks[0] = jnp.where(lat_cut, MASKED, 0.0)
    masks[1] = jnp.where(lev_cut, MASKED, 0.0)
    masks[2] = jnp.where(lat_cut | lev_cut, MASKED, 0.0)

    for copy in xs:
        copy.wait_send()
    for copy in gs:
        copy.start()

    def spread_rows(ref):
        for block in range(2):
            for half in range(2):
                part = ref[block, half].astype(F32).reshape(NT, D)
                at = (2 * block + half) * NT
                for n in range(4):
                    t32[n, at : at + NT, :] = part[:, 128 * n : 128 * n + 128]

    def level_rows(w, k):
        return pl.ds(288 * (w % 2) + LEVELS[w // 2][k], 72, stride=4)

    def window_rows(w):
        halves = []
        for k in range(2):
            halves.append(jnp.concatenate([t32.at[n][level_rows(w, k), :] for n in range(4)], 1))
        return jnp.concatenate(halves, 0)

    for copy in loads[0:14]:
        copy.wait()
    for copy in xs:
        copy.wait_recv()
    gain = gain_ref[...]
    beta = bias_ref[...]
    spread_rows(xw)
    for w in range(WINS):
        rows = slice(w * NT, w * NT + NT)
        x = window_rows(w)
        centred = x - jnp.mean(x, -1, keepdims=True)
        variance = jnp.mean(centred * centred, -1, keepdims=True)
        scale = lax.rsqrt(variance + EPS)
        hat = centred * scale
        x32[rows, :] = hat
        inv[rows, :] = scale
        normed[rows, :] = (hat * gain + beta).astype(BF16)
    normt[...] = normed[...].T

    def project(n, _):
        cols = pl.ds(pl.multiple_of(n * 256, 256), 256)
        qkv[:, cols] = dot(normed[...], wp[:, cols]).astype(BF16)
        return 0

    lax.fori_loop(0, 6, project, 0)

    def rows_at(start, rows):
        return pl.ds(pl.multiple_of(start, 16), rows)

    def core_copy(c, k, src, dst):
        return pltpu.make_async_remote_copy(
            src_ref=src, dst_ref=dst, send_sem=core_s.at[c, k], recv_sem=core_r.at[c, k],
            device_id=other, device_id_type=MESH,
        )

    def core_in(c):
        return core_copy(c, 0, cb.at[c, rows_at((1 - core) * 1024, 1024)], rc0.at[c])

    def core_out(c, arriving):
        half = 1 - core if arriving else core
        return core_copy(c, 1, gb.at[c, rows_at(core * 1024, 1024)], gb.at[c, rows_at(half * 1024, 1024)])

    def mine(c):
        return gb.at[c, rows_at(core * 1024 + me * 16, 16)]

    def scatter_copy(c, device, to):
        return pltpu.make_async_remote_copy(
            src_ref=b1.at[c, to], dst_ref=rs.at[c, me], send_sem=rs_s.at[c], recv_sem=rs_r.at[c],
            device_id=device, device_id_type=MESH,
        )

    def gather_copy(c, device):
        return pltpu.make_async_remote_copy(
            src_ref=mine(c), dst_ref=mine(c), send_sem=ag_s.at[c], recv_sem=ag_r.at[c],
            device_id=device, device_id_type=MESH,
        )

    def all_of(ref, send_sem, recv_sem):
        return pltpu.make_async_remote_copy(
            src_ref=ref, dst_ref=ref, send_sem=send_sem, recv_sem=recv_sem, device_id=other, device_id_type=MESH
        )

    def all_scattered(c):
        return all_of(rs.at[c, pl.ds(0, 63)], rs_s.at[c], rs_r.at[c])

    def all_gathered(c):
        return all_of(gb.at[c, pl.ds(0, 1008)], ag_s.at[c], ag_r.at[c])

    def chunk_done(c):
        core_in(c).start()

    def scatter(c):
        core_in(c).wait_recv()
        own = cb[c, rows_at(core * 1024, 1024), :].astype(F32)
        b1[c] = (own + rc0[c].astype(F32)).astype(BF16).reshape(64, 16, 128)
        rs[c, me] = b1[c, me]
        all_chips(lambda device, to: scatter_copy(c, device, to).start())

    def gather(c):
        all_scattered(c).wait_recv()
        total = jnp.sum(rs[c].astype(F32), 0)
        gb[c, rows_at(core * 1024 + me * 16, 16), :] = total.astype(BF16)
        all_chips(lambda device, _: gather_copy(c, device).start())

    def share(c):
        all_gathered(c).wait_recv()
        core_out(c, False).start()

    def place_in(c):
        return ((xx, zz * 4 + yy), (yy, xx * 4 + zz), (zz, yy * 4 + xx))[c]

    def plane_chips(c, act):
        for d in range(1, 16):
            i, j = divmod(d, 4)
            if c == 0:
                y = turned(yy, j, 4)
                act((layer_lon[i] + y * 4 + xx, layer_lat[i]), turned(zz, i, 4) * 4 + y)
            elif c == 1:
                x = turned(xx, i, 4)
                act((layer_lon[j] + yy * 4 + x, layer_lat[j]), x * 4 + turned(zz, j, 4))
            else:
                r = turned(yy, i, 4) * 4 + turned(xx, j, 4)
                act((lon - flat + r, lat), r)

    def axis_copies(c, back, arriving):
        a, q = place_in(c)
        out = []
        for d in (1, 2, 3):
            to = turned(a, d, 4)
            if back:
                at = turned(a, 4 - d, 4) if arriving else a
                src = gb.at[c, rows_at(core * 1024 + a * 256, 256)]
                dst = gb.at[c, rows_at(core * 1024 + at * 256, 256)]
            else:
                src = b1.at[c, pl.ds(to * 16, 16)]
                dst = ra.at[c, d - 1]
            k = 3 * back + d - 1
            out.append(
                pltpu.make_async_remote_copy(
                    src_ref=src, dst_ref=dst, send_sem=ax_s.at[c, k], recv_sem=ax_r.at[c, k],
                    device_id=peer("xyz"[c], d), device_id_type=MESH,
                )
            )
        return out

    def piece(c):
        a, q = place_in(c)
        return rows_at(core * 1024 + a * 256 + q * 16, 16)

    def to_plane(c, back):
        _, q = place_in(c)

        def one(device, to):
            if back:
                src = dst = gb.at[c, piece(c)]
            else:
                src, dst = r1.at[c, to], rs.at[c, q]
            pltpu.make_async_remote_copy(
                src_ref=src, dst_ref=dst,
                send_sem=(ag_s if back else rs_s).at[c], recv_sem=(ag_r if back else rs_r).at[c],
                device_id=device, device_id_type=MESH,
            ).start()

        plane_chips(c, one)

    def plane_scattered(c):
        return all_of(rs.at[c, pl.ds(0, 15)], rs_s.at[c], rs_r.at[c])

    def plane_gathered(c):
        return all_of(gb.at[c, pl.ds(0, 240)], ag_s.at[c], ag_r.at[c])

    def scatter_axis(c):
        core_in(c).wait_recv()
        own = cb[c, rows_at(core * 1024, 1024), :].astype(F32)
        b1[c] = (own + rc0[c].astype(F32)).astype(BF16).reshape(64, 16, 128)
        for copy in axis_copies(c, False, False):
            copy.start()

    def scatter_plane(c):
        a, q = place_in(c)
        for copy in axis_copies(c, False, True):
            copy.wait_recv()
        own = b1[c, pl.ds(a * 16, 16)].astype(F32)
        for d in range(3):
            own = own + ra[c, d].astype(F32)
        r1[c] = own.astype(BF16)
        rs[c, q] = r1[c, q]
        to_plane(c, False)

    def gather_plane(c):
        plane_scattered(c).wait_recv()
        gb[c, piece(c), :] = jnp.sum(rs[c, 0:16].astype(F32), 0).astype(BF16)
        to_plane(c, True)

    def gather_axis(c):
        plane_gathered(c).wait_recv()
        for copy in axis_copies(c, True, False):
            copy.start()

    def share_axis(c):
        for copy in axis_copies(c, True, True):
            copy.wait_recv()
        core_out(c, False).start()

    def out_copy(c):
        return pltpu.make_async_copy(gb.at[c], out_sum.at[c], out_sem.at[1 + c])

    def finish(c):
        core_out(c, True).wait_recv()
        out_copy(c).start()

    low = lax.broadcasted_iota(jnp.int32, (NT, 128), 1) < 64
    zero = jnp.zeros((), BF16)

    def by_head(x):
        return jnp.concatenate([jnp.where(low, x, zero), jnp.where(low, zero, x)], 0)

    def part_of(p, s):
        return pl.ds(pl.multiple_of(p * 384 + 128 * s, 128), 128)

    def forward(p, w):
        rows = slice(w * NT, w * NT + NT)
        s = dot_nt(qkv[rows, part_of(p, 1)], by_head(qkv[rows, part_of(p, 0)] * 0.125)) + bias_t[p]
        if w > 0:
            s = s + masks[w - 1]
        e = jnp.exp(s - jnp.max(s, 0, keepdims=True))
        prob = e * (1.0 / jnp.sum(e, 0, keepdims=True))
        probs[p, w] = prob
        both = dot(qkv[rows, part_of(p, 2)].T, prob.astype(BF16))
        att = jnp.concatenate([both[0:64, 0:NT], both[64:128, NT : 2 * NT]], 0)
        atts[w, pl.ds(pl.multiple_of(p * 128, 128), 128), :] = att.astype(BF16)

    def backward(p, w):
        rows = slice(w * NT, w * NT + NT)
        q2 = by_head(qkv[rows, part_of(p, 0)] * 0.125)
        ga2 = by_head(gatt[rows, pl.ds(pl.multiple_of(p * 128, 128), 128)])
        prob = probs[p, w]
        dp = dot_nt(qkv[rows, part_of(p, 2)], ga2)
        ds = prob * (dp - jnp.sum(prob * dp, 0, keepdims=True))
        if w == 0:
            dsum[p] = ds
        else:
            dsum[p] += ds
        db = ds.astype(BF16)
        dq = (dot(qkv[rows, part_of(p, 1)].T, db) * 0.125).astype(BF16).T
        dqkv[rows, part_of(p, 0)] = jnp.where(low, dq[0:NT], dq[NT : 2 * NT])
        dqkv[rows, part_of(p, 1)] = dot(db, q2).astype(BF16)
        dqkv[rows, part_of(p, 2)] = dot(prob.astype(BF16), ga2).astype(BF16)

    def forward_pair(p, _):
        for w in range(WINS):
            forward(p, w)
        return 0

    lax.fori_loop(0, PAIRS, forward_pair, 0)

    for copy in loads[14:]:
        copy.wait()
    for copy in gs:
        copy.wait_recv()
    spread_rows(gw)
    for w in range(WINS):
        gwin[w * NT : w * NT + NT, :] = window_rows(w).astype(BF16)

    def project_g(n, _):
        cols = pl.ds(pl.multiple_of(n * 256, 256), 256)
        gatt[:, cols] = dot_nt(gwin[...], wproj[cols, :]).astype(BF16)
        return 0

    lax.fori_loop(0, 2, project_g, 0)

    dproj = dot(atts[0], gwin[0:NT, :])
    for w in range(1, WINS):
        dproj = dproj + dot(atts[w], gwin[w * NT : w * NT + NT, :])
    for n in range(4):
        cb[0, 512 * n : 512 * n + 512, :] = dproj[:, 128 * n : 128 * n + 128].astype(BF16)
    chunk_done(0)

    def pair(p, _):
        for w in range(WINS):
            backward(p, w)
            if w == WINS - 1:
                cols = pl.ds(pl.multiple_of(p * 384, 128), 384)
                grads = dot(normt[...], dqkv[:, cols])
                for s in range(3):
                    block = 3 * p + s
                    cb[1 + block // 4, rows_at(block % 4 * 512, 512), :] = grads[:, 128 * s : 128 * s + 128].astype(BF16)

                @pl.when(p >= 1)
                def _():
                    chunk_done(p)

                part = dot_nt(dqkv[:, cols], wp[:, cols])

                @pl.when(p == 0)
                def _():
                    dn[...] = part

                @pl.when(p > 0)
                def _():
                    dn[...] += part

            for c, at, step in STEPS:
                if at % 4 == w:
                    call = {"axis": scatter_axis, "plane": scatter_plane}[step]
                    pl.when(p == at // 4)(functools.partial(call, c))
        return 0

    lax.fori_loop(0, PAIRS, pair, 0)

    for h in range(HEADS):
        one = dsum[h // 2, :, NT * (h % 2) : NT * (h % 2) + NT]
        one = jnp.concatenate([one, jnp.zeros((NT, 256 - NT), F32)], 1)
        for n in range(2):
            bj.at[n][pl.ds(h, NT, stride=8), :] = one[:, 128 * n : 128 * n + 128]
    sh[...] = dot(jnp.concatenate([bj[0], bj[1]], 1), picks((256, 384), 1), lax.Precision.HIGHEST)
    total = jnp.zeros((HEADS, 768), F32)
    rest = jnp.zeros((HEADS, 384), F32)
    for j in range(NT):
        at = place_of(j)
        wide = jnp.concatenate([sh[8 * j : 8 * j + 8, :], rest], 1)
        total = total + (wide if at == 0 else pltpu.roll(wide, at, 1))
    for n in range(6):
        exb[8 * n : 8 * n + 8, :] = total[:, 128 * n : 128 * n + 128]
    dg = jnp.zeros((1, D), F32)
    db = jnp.zeros((1, D), F32)
    for w in range(WINS):
        rows = slice(w * NT, w * NT + NT)
        d = dn[rows, :]
        dg = dg + jnp.sum(d * x32[rows, :], 0, keepdims=True)
        db = db + jnp.sum(d, 0, keepdims=True)
    for n in range(4):
        exb[48 + n : 49 + n, :] = dg[:, 128 * n : 128 * n + 128]
        exb[52 + n : 53 + n, :] = db[:, 128 * n : 128 * n + 128]
    exb[56:64, :] = jnp.zeros((8, 128), F32)

    def small(k, src, dst, device):
        return pltpu.make_async_remote_copy(
            src_ref=src, dst_ref=dst, send_sem=exs.at[k], recv_sem=exr.at[k],
            device_id=device, device_id_type=MESH,
        )

    def small_ring(axis, at, buf, k, arriving):
        src = buf.at[at]
        out = []
        for d in (1, 2, 3):
            dst = buf.at[turned(at, 4 - d, 4) if arriving else at]
            out.append(small(k + d - 1, src, dst, peer(axis, d)))
        return out

    def small_step(axis, at, buf, k):
        for copy in small_ring(axis, at, buf, k, True):
            copy.wait_recv()
        return (buf[0] + buf[1]) + (buf[2] + buf[3])

    first = small(0, exb, exc, other)
    first.start()
    scatter(3)
    gather_plane(0)
    scatter_plane(1)

    for w in range(WINS):
        rows = slice(w * NT, w * NT + NT)
        hat = x32[rows, :]
        g = dn[rows, :] * gain
        m1 = jnp.mean(g, -1, keepdims=True)
        m2 = jnp.mean(g * hat, -1, keepdims=True)
        branch = inv[rows, :] * (g - m1 - hat * m2)
        for k in range(2):
            for n in range(4):
                t32.at[n][level_rows(w, k), :] = branch[72 * k : 72 * k + 72, 128 * n : 128 * n + 128]
    for block in range(2):
        for half in range(2):
            at = (2 * block + half) * NT
            part = jnp.concatenate([t32[n, at : at + NT, :] for n in range(4)], 1)
            yw[block, half] = part.reshape(6, 6, 4, D).astype(BF16)

    def homeward(k, piece):
        rows, cols, at, dlat, dlon = piece
        return pltpu.make_async_remote_copy(
            src_ref=window_part(yw, at),
            dst_ref=grid_part(ret, rows, cols),
            send_sem=ret_s.at[k],
            recv_sem=ret_r.at[k],
            device_id=beside(-dlat, -dlon),
            device_id_type=MESH,
        )

    rets = [homeward(k, piece) for k, piece in enumerate(PIECES)]
    for copy in rets:
        copy.start()
    kept = []
    for k, (rows, cols, at) in enumerate(KEPT):
        kept.append(pltpu.make_async_copy(window_part(yw, at), grid_part(ret, rows, cols), load_sem.at[k]))
        kept[-1].start()

    scatter_plane(2)
    first.wait_recv()
    exx[xx] = exb[...] + exc[...]
    for copy in small_ring("x", xx, exx, 1, False):
        copy.start()
    gather_plane(1)
    gather_axis(0)
    gather_plane(2)
    exy[yy] = small_step("x", xx, exx, 1)
    for copy in small_ring("y", yy, exy, 4, False):
        copy.start()
    gather(3)

    for copy in kept:
        copy.wait()
    for copy in rets:
        copy.wait_recv()
    gnat[...] = (gnat[...].astype(F32) + ret[...].astype(F32)).astype(BF16)
    token_copy = pltpu.make_async_copy(gnat, out_tok, out_sem.at[0])
    token_copy.start()

    share_axis(0)
    gather_axis(1)
    gather_axis(2)
    exz[zz] = small_step("y", yy, exy, 4)
    for copy in small_ring("z", zz, exz, 7, False):
        copy.start()
    finish(0)
    share(3)
    share_axis(1)
    share_axis(2)
    finish(3)
    out_small[...] = small_step("z", zz, exz, 7) * FACTOR
    finish(1)
    finish(2)

    for copy in gs + rets + [first]:
        copy.wait_send()
    for axis, at, buf, k in (("x", xx, exx, 1), ("y", yy, exy, 4), ("z", zz, exz, 7)):
        for copy in small_ring(axis, at, buf, k, False):
            copy.wait_send()
    for c in range(PAIRS):
        core_in(c).wait_send()
        if c == 3:
            all_scattered(c).wait_send()
            all_gathered(c).wait_send()
        else:
            plane_scattered(c).wait_send()
            plane_gathered(c).wait_send()
            for copy in axis_copies(c, False, False) + axis_copies(c, True, False):
                copy.wait_send()
        core_out(c, False).wait_send()
        out_copy(c).wait()
    token_copy.wait()


def finish_kernel(tok_in, sum_hbm, small, out_tok, out_wqkv, out_wproj, out_gain, out_beta, out_table, gb, ow, op, tok, sems):
    tokens_in = pltpu.make_async_copy(tok_in, tok, sems.at[0])
    tokens = pltpu.make_async_copy(tok, out_tok, sems.at[21])
    loads = [pltpu.make_async_copy(sum_hbm.at[c], gb.at[c], sems.at[1 + c]) for c in range(PAIRS)]
    for copy in loads:
        copy.start()
    tokens_in.start()
    outs = []
    for c in range(PAIRS):
        loads[c].wait()
        for n in range(4):
            part = gb[c, 512 * n : 512 * n + 512, :].astype(F32) * FACTOR
            if c == 0:
                op[:, 128 * n : 128 * n + 128] = part
            else:
                pair, kind = divmod(4 * (c - 1) + n, 3)
                cols = slice(512 * kind + 128 * pair, 512 * kind + 128 * pair + 128)
                ow[:, cols] = part
                outs.append(pltpu.make_async_copy(ow.at[:, cols], out_wqkv.at[:, cols], sems.at[5 + 4 * c + n]))
                outs[-1].start()
        if c == 0:
            outs.append(pltpu.make_async_copy(op, out_wproj, sems.at[5]))
            outs[-1].start()
    for n in range(5):
        out_table[:, 128 * n : 128 * n + 128] = small[8 * n : 8 * n + 8, :]
    out_table[:, 640:RELS] = small[40:48, 0 : RELS - 640]
    for n in range(4):
        out_gain[:, 128 * n : 128 * n + 128] = small[48 + n : 49 + n, :]
        out_beta[:, 128 * n : 128 * n + 128] = small[52 + n : 53 + n, :]
    tokens_in.wait()
    tokens.start()
    for copy in outs + [tokens]:
        copy.wait()


def shards(tokens, grad_output, norm_gain, norm_bias, w_qkv, w_proj, rel_bias):
    any_space = pl.BlockSpec(memory_space=pl.ANY)
    vmem = pl.BlockSpec(memory_space=pltpu.VMEM)
    dma = pltpu.SemaphoreType.DMA
    by_window = (2, 2, 6, 6, 4, D)
    by_grid = (12, 12, 4, D)
    scratch = [
        pltpu.VMEM(by_window, BF16),
        pltpu.VMEM(by_window, BF16),
        pltpu.VMEM(by_grid, BF16),
        pltpu.VMEM(by_window, BF16),
        pltpu.VMEM(by_grid, BF16),
        pltpu.VMEM((D, 3 * D), BF16),
        pltpu.VMEM((D, D), BF16),
        pltpu.VMEM((TOK, D), F32),
        pltpu.VMEM((4, TOK, 128), F32),
        pltpu.VMEM((TOK, 1), F32),
        pltpu.VMEM((TOK, D), BF16),
        pltpu.VMEM((D, TOK), BF16),
        pltpu.VMEM((TOK, 3 * D), BF16),
        pltpu.VMEM((TOK, D), BF16),
        pltpu.VMEM((TOK, D), BF16),
        pltpu.VMEM((TOK, 3 * D), BF16),
        pltpu.VMEM((TOK, D), F32),
        pltpu.VMEM((HEADS, 768), F32),
        pltpu.VMEM((HEADS * NT, 384), F32),
        pltpu.VMEM((2, HEADS * NT, 128), F32),
        pltpu.VMEM((PAIRS, NT, 2 * NT), F32),
        pltpu.VMEM((3, NT, 2 * NT), F32),
        pltpu.VMEM((PAIRS, NT, 2 * NT), F32),
        pltpu.VMEM((PAIRS, WINS, NT, 2 * NT), F32),
        pltpu.VMEM((WINS, D, NT), BF16),
        pltpu.VMEM((PAIRS, 2048, 128), BF16),
        pltpu.VMEM((PAIRS, 1024, 128), BF16),
        pltpu.VMEM((PAIRS, 64, 16, 128), BF16),
        pltpu.VMEM((3, 3, 16, 16, 128), BF16),
        pltpu.VMEM((3, 16, 16, 128), BF16),
        pltpu.VMEM((PAIRS, 64, 16, 128), BF16),
        pltpu.VMEM((PAIRS, 2048, 128), BF16),
        pltpu.VMEM((64, 128), F32),
        pltpu.VMEM((64, 128), F32),
        pltpu.VMEM((4, 64, 128), F32),
        pltpu.VMEM((4, 64, 128), F32),
        pltpu.VMEM((4, 64, 128), F32),
        dma((18,)),
        dma((8,)),
        dma((8,)),
        dma((4,)),
        dma((4,)),
        dma((PAIRS, 2)),
        dma((PAIRS, 2)),
        dma((3, 6)),
        dma((3, 6)),
        dma((PAIRS,)),
        dma((PAIRS,)),
        dma((PAIRS,)),
        dma((PAIRS,)),
        dma((10,)),
        dma((10,)),
        dma((5,)),
    ]
    tok_out, summed, small = pl.pallas_call(
        kernel,
        out_shape=(
            jax.ShapeDtypeStruct(by_grid, BF16),
            jax.ShapeDtypeStruct((PAIRS, 2048, 128), BF16),
            jax.ShapeDtypeStruct((64, 128), F32),
        ),
        in_specs=[any_space, any_space, vmem, vmem, any_space, any_space, vmem],
        out_specs=(any_space, any_space, vmem),
        scratch_shapes=scratch,
        compiler_params=pltpu.CompilerParams(
            collective_id=0, has_side_effects=True, vmem_limit_bytes=56 * 1024 * 1024
        ),
    )(
        tokens.transpose(1, 2, 0, 3),
        grad_output.transpose(1, 2, 0, 3),
        norm_gain[None],
        norm_bias[None],
        w_qkv,
        w_proj,
        rel_bias,
    )
    out = pl.pallas_call(
        finish_kernel,
        out_shape=(
            jax.ShapeDtypeStruct(by_grid, BF16),
            jax.ShapeDtypeStruct((D, 3 * D), F32),
            jax.ShapeDtypeStruct((D, D), F32),
            jax.ShapeDtypeStruct((1, D), F32),
            jax.ShapeDtypeStruct((1, D), F32),
            jax.ShapeDtypeStruct((HEADS, RELS), F32),
        ),
        in_specs=[any_space, any_space, vmem],
        out_specs=(any_space, any_space, any_space, vmem, vmem, vmem),
        scratch_shapes=[
            pltpu.VMEM((PAIRS, 2048, 128), BF16),
            pltpu.VMEM((D, 3 * D), F32),
            pltpu.VMEM((D, D), F32),
            pltpu.VMEM(by_grid, BF16),
            dma((22,)),
        ],
        compiler_params=pltpu.CompilerParams(vmem_limit_bytes=60 * 1024 * 1024),
    )(tok_out, summed, small)
    return out[0].transpose(2, 0, 1, 3), out[1], out[2], out[3][0], out[4][0], out[5]


def solution(mesh):
    grid = P(None, "lat", "lon", None)
    return jax.shard_map(
        shards,
        mesh=mesh,
        in_specs=(grid, grid, P(), P(), P(), P(), P()),
        out_specs=(grid, P(), P(), P(), P(), P()),
        check_vma=False,
    )
```

time: 398 us -> 77.2 us (0.19); the launches traced: 390 us -> 76.9 us
  local copies, waits for them, and re-layouts: 119 us -> 0 us
  matrix products: 86.9 us -> 0 us
  Pallas kernels: 0 us -> 76.3 us
  waiting for transfers between devices: 64.8 us -> 0 us
  blocking collectives: 63 us -> 0 us
  other arithmetic: 29.4 us -> 0 us
  between operations: 15 us -> 0.64 us
  starting transfers between devices: 12.1 us -> 0 us
    dot_general x17 -> x0, matrix products: 86.9 us -> none  [the longest x3 25.2 us: window_backward(): jnp.einsum('hxyz,psx,qty,ruz->hpqrstu', bias_table, hot_lev, hot_lat, hot...]
    pallas_call x0 -> x2, Pallas kernels: none -> 76.3 us  [the longest x1 71.3 us: shards(): pl.pallas_call(kernel, out_shape=(jax.ShapeDtypeStruct(by_grid, BF16), ja...]
    psum x1 -> x0, blocking collectives: 63 us -> none  [shards(): summed = lax.psum((d_wqkv, d_proj, d_gain, d_beta, d_table), ('lon', 'lat'))]
    psum x1 -> x0, waiting for transfers between devices: 50.7 us -> none  [shards(): summed = lax.psum((d_wqkv, d_proj, d_gain, d_beta, d_table), ('lon', 'lat'))]
    reshape x13 -> x0, local copies, waits for them, and re-layouts: 45 us -> none  [the longest x2 21.6 us: window_backward(): jnp.sum(d_scores, 0)]
    add x2 -> x0, local copies, waits for them, and re-layouts: 23.1 us -> none  [window_backward(): jnp.einsum('bihc,bjhc->bhij', query_h, key_h, preferred_element_type=f32)]
    ppermute x6 -> x0, waiting for transfers between devices: 14 us -> none  [passed_along(): return lax.ppermute(block, axis, route)]
    convert_element_type x7 -> x0, local copies, waits for them, and re-layouts: 12.4 us -> none  [the longest x4 8.97 us: window_backward(): x_full = x_win.astype(f32)]
  transfers between devices with their start and end apart: 7 -> 0, of which waited for: 3 -> 0; matrix products, arithmetic and copies ran while one was open for 30% -> 0% of each run, Pallas kernels for 0% -> 0%
where the time goes in v2:
time: 77.2 us; the launch traced here: 76.9 us
  Pallas kernels  76.3 us (99%)
    pallas_call x1, Pallas kernels, shards(): pl.pallas_call(kernel, out_shape=(jax.ShapeDtypeStruct(by_grid, BF16), ja...  71.3 us
    pallas_call x1, Pallas kernels, shards(): pl.pallas_call(finish_kernel, out_shape=(jax.ShapeDtypeStruct(by_grid, BF...  4.94 us

profile of v2, /device:TPU:1, one launch (start us, length us, event | category | flops | bytes accessed | tf_op | source)
XLA Modules:
  0.0 76.9 jit_solution(16511593071575880581)
XLA Ops:
  0.6 71.3 %shard_map.118 = (bf16[12,12,4,512]{3,2,1,0:T(4,128)(2,1)}, bf16[4,2048,128]{2,1,0:T(8,128)(2,1)}, f32[64,128]{1,0:T(8,128)}) custom-call(bf16[12,12,4,512]{3,2,1,0:T(4,128)(2,1)} %bitcast.7, bf16[12,12,4,512]{3,2,1,0:T(4,128)(2,1)} %bitcast.8, f32[1,512]{1,0:T(1,128)} %bitcast.9, f32[1,512]{1,0:T(1,128)} %bitcast.10, bf16[512,1536]{1,0:T(8,128)(2,1)} %wqkv_hbm.1, ...), custom_call_target="tpu_custom_call" | custom-call | tf_op jit(solution)/shard_map/pallas_call | solution.py:740
  72.0 4.9 %shard_map.119 = (bf16[12,12,4,512]{3,2,1,0:T(4,128)(2,1)}, f32[512,1536]{1,0:T(8,128)}, f32[512,512]{1,0:T(8,128)}, f32[1,512]{1,0:T(1,128)}, f32[1,512]{1,0:T(1,128)}, /*index=5*/f32[8,759]{1,0:T(8,128)}) custom-call(bf16[12,12,4,512]{3,2,1,0:T(4,128)(2,1)} %get-tuple-element.15.tok_in, bf16[4,2048,128]{2,1,0:T(8,128)(2,1)} %get-tuple-element.16.sum_hbm, ...), custom_call_target="tpu_custom_call" | custom-call | tf_op jit(solution)/shard_map/pallas_call | solution.py:762

commit v3 on v2

--- a/solution.py
+++ b/solution.py
@@ -523,7 +523,6 @@
     for n in range(4):
         exb[48 + n : 49 + n, :] = dg[:, 128 * n : 128 * n + 128]
         exb[52 + n : 53 + n, :] = db[:, 128 * n : 128 * n + 128]
-    exb[56:64, :] = jnp.zeros((8, 128), F32)
 
     def small(k, src, dst, device):
         return pltpu.make_async_remote_copy(
@@ -643,35 +642,38 @@
 
 def finish_kernel(tok_in, sum_hbm, small, out_tok, out_wqkv, out_wproj, out_gain, out_beta, out_table, gb, ow, op, tok, sems):
     tokens_in = pltpu.make_async_copy(tok_in, tok, sems.at[0])
-    tokens = pltpu.make_async_copy(tok, out_tok, sems.at[21])
-    loads = [pltpu.make_async_copy(sum_hbm.at[c], gb.at[c], sems.at[1 + c]) for c in range(PAIRS)]
-    for copy in loads:
-        copy.start()
-    tokens_in.start()
+    tokens = pltpu.make_async_copy(tok, out_tok, sems.at[1])
+    loads = []
+    for k in range(16):
+        part = pl.ds(512 * (k % 4), 512)
+        loads.append(pltpu.make_async_copy(sum_hbm.at[k // 4, part], gb.at[k // 4, part], sems.at[2 + k]))
+    for k in range(16):
+        loads[k].start()
+        if k == 7:
+            tokens_in.start()
     outs = []
-    for c in range(PAIRS):
-        loads[c].wait()
-        for n in range(4):
-            part = gb[c, 512 * n : 512 * n + 512, :].astype(F32) * FACTOR
-            if c == 0:
-                op[:, 128 * n : 128 * n + 128] = part
-            else:
-                pair, kind = divmod(4 * (c - 1) + n, 3)
-                cols = slice(512 * kind + 128 * pair, 512 * kind + 128 * pair + 128)
-                ow[:, cols] = part
-                outs.append(pltpu.make_async_copy(ow.at[:, cols], out_wqkv.at[:, cols], sems.at[5 + 4 * c + n]))
-                outs[-1].start()
-        if c == 0:
-            outs.append(pltpu.make_async_copy(op, out_wproj, sems.at[5]))
-            outs[-1].start()
+    for k in range(16):
+        loads[k].wait()
+        part = gb[k // 4, 512 * (k % 4) : 512 * (k % 4) + 512, :].astype(F32) * FACTOR
+        if k < 4:
+            op[:, 128 * k : 128 * k + 128] = part
+            cols = slice(128 * k, 128 * k + 128)
+            outs.append(pltpu.make_async_copy(op.at[:, cols], out_wproj.at[:, cols], sems.at[18 + k]))
+        else:
+            pair, kind = divmod(k - 4, 3)
+            cols = slice(512 * kind + 128 * pair, 512 * kind + 128 * pair + 128)
+            ow[:, cols] = part
+            outs.append(pltpu.make_async_copy(ow.at[:, cols], out_wqkv.at[:, cols], sems.at[18 + k]))
+        outs[-1].start()
+        if k == 11:
+            tokens_in.wait()
+            tokens.start()
     for n in range(5):
         out_table[:, 128 * n : 128 * n + 128] = small[8 * n : 8 * n + 8, :]
     out_table[:, 640:RELS] = small[40:48, 0 : RELS - 640]
     for n in range(4):
         out_gain[:, 128 * n : 128 * n + 128] = small[48 + n : 49 + n, :]
         out_beta[:, 128 * n : 128 * n + 128] = small[52 + n : 53 + n, :]
-    tokens_in.wait()
-    tokens.start()
     for copy in outs + [tokens]:
         copy.wait()
 
@@ -715,11 +717,11 @@
         pltpu.VMEM((3, 16, 16, 128), BF16),
         pltpu.VMEM((PAIRS, 64, 16, 128), BF16),
         pltpu.VMEM((PAIRS, 2048, 128), BF16),
-        pltpu.VMEM((64, 128), F32),
-        pltpu.VMEM((64, 128), F32),
-        pltpu.VMEM((4, 64, 128), F32),
-        pltpu.VMEM((4, 64, 128), F32),
-        pltpu.VMEM((4, 64, 128), F32),
+        pltpu.VMEM((56, 128), F32),
+        pltpu.VMEM((56, 128), F32),
+        pltpu.VMEM((4, 56, 128), F32),
+        pltpu.VMEM((4, 56, 128), F32),
+        pltpu.VMEM((4, 56, 128), F32),
         dma((18,)),
         dma((8,)),
         dma((8,)),
@@ -742,7 +744,7 @@
         out_shape=(
             jax.ShapeDtypeStruct(by_grid, BF16),
             jax.ShapeDtypeStruct((PAIRS, 2048, 128), BF16),
-            jax.ShapeDtypeStruct((64, 128), F32),
+            jax.ShapeDtypeStruct((56, 128), F32),
         ),
         in_specs=[any_space, any_space, vmem, vmem, any_space, any_space, vmem],
         out_specs=(any_space, any_space, vmem),
@@ -776,7 +778,7 @@
             pltpu.VMEM((D, 3 * D), F32),
             pltpu.VMEM((D, D), F32),
             pltpu.VMEM(by_grid, BF16),
-            dma((22,)),
+            dma((34,)),
         ],
         compiler_params=pltpu.CompilerParams(vmem_limit_bytes=60 * 1024 * 1024),
     )(tok_out, summed, small)

time: 77.2 us -> 76.8 us (level)
  no operation moved by 1% of the time
where the time goes in v3:
time: 76.8 us; the launch traced here: 76.6 us
  Pallas kernels  75.9 us (99%)
    pallas_call x1, Pallas kernels, shards(): pl.pallas_call(kernel, out_shape=(jax.ShapeDtypeStruct(by_grid, BF16), ja...  71.1 us
    pallas_call x1, Pallas kernels, shards(): pl.pallas_call(finish_kernel, out_shape=(jax.ShapeDtypeStruct(by_grid, BF...  4.78 us

profile of v3, /device:TPU:1, one launch (start us, length us, event | category | flops | bytes accessed | tf_op | source)
XLA Modules:
  0.0 76.6 jit_solution(1900335118354000347)
XLA Ops:
  0.6 71.1 %shard_map.118 = (bf16[12,12,4,512]{3,2,1,0:T(4,128)(2,1)}, bf16[4,2048,128]{2,1,0:T(8,128)(2,1)}, f32[56,128]{1,0:T(8,128)}) custom-call(bf16[12,12,4,512]{3,2,1,0:T(4,128)(2,1)} %bitcast.7, bf16[12,12,4,512]{3,2,1,0:T(4,128)(2,1)} %bitcast.8, f32[1,512]{1,0:T(1,128)} %bitcast.9, f32[1,512]{1,0:T(1,128)} %bitcast.10, bf16[512,1536]{1,0:T(8,128)(2,1)} %wqkv_hbm.1, ...), custom_call_target="tpu_custom_call" | custom-call | tf_op jit(solution)/shard_map/pallas_call | solution.py:742
  71.8 4.8 %shard_map.119 = (bf16[12,12,4,512]{3,2,1,0:T(4,128)(2,1)}, f32[512,1536]{1,0:T(8,128)}, f32[512,512]{1,0:T(8,128)}, f32[1,512]{1,0:T(1,128)}, f32[1,512]{1,0:T(1,128)}, /*index=5*/f32[8,759]{1,0:T(8,128)}) custom-call(bf16[12,12,4,512]{3,2,1,0:T(4,128)(2,1)} %get-tuple-element.15.tok_in, bf16[4,2048,128]{2,1,0:T(8,128)(2,1)} %get-tuple-element.16.sum_hbm, ...), custom_call_target="tpu_custom_call" | custom-call | tf_op jit(solution)/shard_map/pallas_call | solution.py:764
